TPU v7x, 32 devices: a whole 2x2x4 slice. The times are simulated.
32 devices in a mesh: tile: 8 (over z, y), spec: 4 (over x, core).
Axes of the slice: x: 2, y: 2, z: 4, core: 2. Of those that a mesh axis runs over, the one named last changes fastest.
Arguments:
- grad_columns: bfloat16 [8192, 512], P('tile', 'spec'), may hold values from -6 to 6
- grad_flux: float32 [16, 8192], P('spec', 'tile'), may hold values from -6 to 6
- remap_part: int32 [8192, 4], P('tile'), may hold values from 0 to 7, all different within a row; in each aligned block of 1024 rows (0 to 1023, 1024 to 2047, ...) at most 1024 rows name the same one
- remap_slot: int32 [8192, 4], P('tile'), may hold values from 0 to 1023
- remap_weight: float32 [8192, 4], P('tile'), may hold values from 0.2 to 1
- col_count: int32 [8], P('tile'), may hold values from 341 to 1024, as said below
- neighbors: int32 [8192, 4], P('tile'), may hold values from 0 to 1279, as said below
- kappa: float32 [16], P('spec'), may hold values from 0.03 to 0.2
- thickness: float32 [16, 32], P('spec'), may hold values from 0.2 to 2
- vertical: bfloat16 [16, 32, 32], P('spec'), may hold values from -1 to 1
- reaction: bfloat16 [16, 16], P(None, 'spec'), may hold values from -1.5 to 1.5
Outputs:
- grad_state: bfloat16 [8192, 512], P('tile', 'spec')
- grad_bottom: float32 [16, 8192], P('spec', 'tile')
Inputs may be any that keep to these rules, and one draw needn't show every extreme that they name: `remap_part`: each coarse cell names 4 different partitions; the entries of the cells of one tile (1024 cells) name one partition at most 1024 times. `col_count`: live counts of partitions differ up to threefold; one partition holds 1024 live columns and one holds 341. `neighbors`: row p * 1024 + i lists the codes of 4 neighbours of slot i of partition p; every named slot is live; the first partition names no previous and the last no next partition.
All inputs are finite; a program needn't handle non-finite values.
Results may differ from a plain program's by a relative error of at most 0.008.
Values may be sent and summed in bfloat16 or wider, within the bound.
No kernel may reach another device: no remote copies, remote signals or barrier semaphores. Data moves between devices by JAX's collectives and lax.ppermute only.
A program may use at most 128 MiB of HBM per device.

v0:
```python
import functools

import jax
import jax.numpy as jnp
from jax import lax
from jax.experimental import pallas as pl
from jax.experimental.pallas import tpu as pltpu
from jax.sharding import PartitionSpec as P

SUB = 4
LANES = 128
WIDE = 256
ROWS = 32
F32 = jnp.float32
BF16 = jnp.bfloat16
VMEM = pl.BlockSpec(memory_space=pltpu.VMEM)
SMEM = pl.BlockSpec(memory_space=pltpu.SMEM)
LIMIT = 48 * 1024 * 1024


def shifted(block, axis, distance):
    devices = range(lax.axis_size(axis))
    route = [(i - distance, i) for i in devices if i - distance in devices]
    return lax.ppermute(block, axis, route)


def call(kernel, outs, specs, scratch=(), flops=0, moved=0):
    return pl.pallas_call(
        kernel,
        out_shape=outs,
        in_specs=specs,
        out_specs=[VMEM] * len(outs),
        scratch_shapes=scratch,
        compiler_params=pltpu.CompilerParams(vmem_limit_bytes=LIMIT),
        cost_estimate=pl.CostEstimate(flops=flops, bytes_accessed=moved, transcendentals=0),
    )


def nt(a, b, precision=None):
    return lax.dot_general(
        a, b, (((1,), (1,)), ((), ())), precision=precision, preferred_element_type=F32
    )


def nn(a, b, precision=None):
    return lax.dot_general(
        a, b, (((1,), (0,)), ((), ())), precision=precision, preferred_element_type=F32
    )


def row_ids(rows, cols):
    return lax.broadcasted_iota(jnp.int32, (rows, cols), 0)


def chosen(key, rows):
    hit = row_ids(rows, key.shape[1]) == key
    return jnp.where(hit, 1.0, 0.0).astype(BF16)


def rate_column(kappa_ref, rows, group):
    ids = row_ids(rows, 1)
    out = jnp.zeros((rows, 1), F32)
    for s in range(kappa_ref.shape[0]):
        out = jnp.where((ids // group) % kappa_ref.shape[0] == s, kappa_ref[s], out)
    return out


def prepare(
    count_ref, gc_ref, vert_ref, thick_ref, flux_ref, part_ref, slot_ref, weight_ref, nbr_ref,
    payload_ref, w_ref, tv_ref,
):
    species, layers, _ = vert_ref.shape
    width = species * layers
    col_max = gc_ref.shape[0]
    v = vert_ref[...].astype(F32).reshape(width, layers)
    v = jnp.concatenate([v] * species, axis=1)
    rows = row_ids(width, width) // layers
    cols = lax.broadcasted_iota(jnp.int32, (width, width), 1) // layers
    vt = jnp.where(rows == cols, v, 0.0).T
    hi = lax.Precision.HIGHEST
    v2 = nn(vt, vt, hi)
    v4 = nn(v2, v2, hi)
    th = jnp.concatenate([thick_ref[s : s + 1, :] for s in range(species)], axis=1)
    tv_ref[...] = jnp.sum(v4 * th, axis=1, keepdims=True)
    live = lax.broadcasted_iota(jnp.int32, (1, col_max), 1) < count_ref[0]
    w = jnp.where(live, nt(v4.astype(BF16), gc_ref[...]), 0.0)
    w_ref[...] = w
    top = [w[s * layers : s * layers + 1, :] for s in range(species)]
    slot = slot_ref[...]
    nbr = nbr_ref[...]
    code = (nbr // LANES) * 4 + slot // WIDE
    pieces = top + [
        flux_ref[...],
        weight_ref[...],
        part_ref[...].astype(F32),
        (slot % WIDE).astype(F32),
        code.astype(F32),
        (nbr % LANES).astype(F32),
        jnp.where(live, 1.0, 0.0),
        jnp.zeros((ROWS - 7 * 4 - 1, col_max), F32),
    ]
    payload_ref[...] = jnp.concatenate(pieces, axis=0).astype(BF16)


def spread_out(x, kcol, counts):
    ext = nt((kcol * x).astype(BF16), counts)
    col_max = x.shape[1]
    return (
        (1.0 - 4.0 * kcol) * x + ext[:, :col_max],
        ext[:, col_max : col_max + LANES].astype(BF16),
        ext[:, col_max + LANES :].astype(BF16),
    )


def first_step(kappa_ref, nbr_ref, w_ref, counts_ref, x_ref, prev_ref, next_ref):
    width, col_max = w_ref.shape
    nbr = nbr_ref[...]
    high, low = nbr // LANES, nbr % LANES
    for h in range(counts_ref.shape[0] // LANES):
        block = jnp.zeros((LANES, col_max), F32)
        for n in range(nbr.shape[0]):
            key = jnp.where(high[n : n + 1] == h, low[n : n + 1], -1)
            block = block + jnp.where(row_ids(LANES, col_max) == key, 1.0, 0.0)
        counts_ref[h * LANES : (h + 1) * LANES, :] = block.astype(BF16)
    kcol = rate_column(kappa_ref, width, width // kappa_ref.shape[0])
    x_ref[...], prev_ref[...], next_ref[...] = spread_out(w_ref[...], kcol, counts_ref[...])


def joined(part, from_prev, from_next):
    return jnp.concatenate(
        [
            part[:, :LANES] + from_prev.astype(F32),
            part[:, LANES : 2 * LANES] + from_next.astype(F32),
            part[:, 2 * LANES :],
        ],
        axis=1,
    )


def next_step(kappa_ref, counts_ref, part_ref, from_prev, from_next, x_ref, prev_ref, next_ref):
    width = part_ref.shape[0]
    x = joined(part_ref[...], from_prev[...], from_next[...])
    kcol = rate_column(kappa_ref, width, width // kappa_ref.shape[0])
    x_ref[...], prev_ref[...], next_ref[...] = spread_out(x, kcol, counts_ref[...])


def chain(tiles, kappa_ref, tv_ref, data_ref, out_ref, x_ref, table_ref):
    col_max = data_ref.shape[1]
    species = kappa_ref.shape[0]
    layers = tv_ref.shape[0] // species
    subs = col_max // WIDE
    groups = tiles * subs // 2
    second = jnp.where(row_ids(8, 1) >= 4, 1, 0)

    table_ref[...] = jnp.zeros_like(table_ref)

    def gather(q, carry):
        block = data_ref[pl.ds(pl.multiple_of(q * ROWS, ROWS), ROWS), :].astype(F32)
        ints = block[12:28].astype(jnp.int32)
        part, low, code = ints[0:4], ints[4:8], ints[8:12]
        high = part * subs + (code & 3)
        total = jnp.zeros(table_ref.shape, F32)
        for r in range(4):
            value = block[4:8] * block[8 + r : 9 + r]
            value = jnp.concatenate([value, value], axis=0)
            key = high[r : r + 1] - second
            rows = [jnp.where(key == 2 * g, value, 0.0) for g in range(groups)]
            total = total + nt(
                jnp.concatenate(rows, axis=0).astype(BF16), chosen(low[r : r + 1], WIDE)
            )
        table_ref[...] += total
        return carry

    lax.fori_loop(0, tiles, gather, 0)

    tv0 = jnp.concatenate([tv_ref[s * layers : s * layers + 1, :] for s in range(4)], axis=0)
    for q in range(tiles):
        live = data_ref[q * ROWS + 28 : q * ROWS + 29, :].astype(F32)
        inj = [table_ref[(q * subs + h) * 4 : (q * subs + h) * 4 + 4, :] for h in range(subs)]
        inj = jnp.concatenate(inj, axis=1) * live
        top = data_ref[q * ROWS : q * ROWS + 4, :].astype(F32)
        x_ref[0, q] = jnp.concatenate([top + tv0 * inj, inj], axis=0)

    kcol = rate_column(kappa_ref, 8, 1)
    high_count = col_max // LANES + 2
    pairs = high_count // 2
    second16 = jnp.where(row_ids(16, 1) >= 8, 1, 0)
    for step in range(SUB):
        here, there = step % 2, (step + 1) % 2
        for q in range(tiles):
            x_ref[there, q] = (1.0 - 4.0 * kcol) * x_ref[here, q]

        def apply(q, carry):
            block = data_ref[pl.ds(pl.multiple_of(q * ROWS, ROWS), ROWS), :].astype(F32)
            ints = block[20:28].astype(jnp.int32)
            high, low = ints[0:4] // 4, ints[4:8]
            value = kcol * x_ref[here, q]
            value = jnp.concatenate([value, value], axis=0)
            total = jnp.zeros((high_count * 8, LANES), F32)
            for n in range(4):
                key = high[n : n + 1] - second16
                rows = [jnp.where(key == 2 * g, value, 0.0) for g in range(pairs)]
                total = total + nt(
                    jnp.concatenate(rows, axis=0).astype(BF16), chosen(low[n : n + 1], LANES)
                )
            own = [total[h * 8 : h * 8 + 8] for h in range(high_count - 2)]
            x_ref[there, q] += jnp.concatenate(own, axis=1)
            before, after = jnp.maximum(q - 1, 0), jnp.minimum(q + 1, tiles - 1)
            to_prev = jnp.where(q > 0, total[8 * (high_count - 2) : 8 * (high_count - 1)], 0.0)
            to_next = jnp.where(q < tiles - 1, total[8 * (high_count - 1) :], 0.0)
            x_ref[there, before, :, LANES : 2 * LANES] += to_prev
            x_ref[there, after, :, :LANES] += to_next
            return carry

        lax.fori_loop(0, tiles, apply, 0)
    out_ref[...] = x_ref[SUB % 2]


def finish(
    tiles, part_ref, from_prev, from_next, tv_ref, chain_ref, rpart_ref, slot_ref, weight_ref,
    out_ref, y_ref, u_ref,
):
    width, col_max = part_ref.shape
    species = 4
    layers = width // species
    me = lax.axis_index("tile")
    x = joined(part_ref[...], from_prev[...], from_next[...])
    inj = chain_ref[me][4:8]
    inj = jnp.concatenate(
        [jnp.broadcast_to(inj[s : s + 1], (layers, col_max)) for s in range(species)], axis=0
    )
    out_ref[:width, :] = (x + tv_ref[...] * inj).astype(BF16)
    subs = col_max // WIDE
    half = tiles * subs // 2
    for i in range(half):
        first, other = i, i + half
        a = chain_ref[first // subs, 0:4, (first % subs) * WIDE : (first % subs + 1) * WIDE]
        b = chain_ref[other // subs, 0:4, (other % subs) * WIDE : (other % subs + 1) * WIDE]
        y_ref[i * 8 : i * 8 + 8, :] = jnp.concatenate([a, b], axis=0)
    y = y_ref[...].astype(BF16)
    slot = slot_ref[...]
    high = rpart_ref[...] * subs + slot // WIDE
    low = slot % WIDE
    offset = jnp.where(row_ids(8, 1) >= 4, half, 0)
    total = jnp.zeros((8, col_max), F32)
    for r in range(4):
        u_ref[...] = nn(y, chosen(low[r : r + 1], WIDE))
        key = high[r : r + 1] - offset
        found = jnp.zeros((8, col_max), F32)
        for i in range(half):
            found = jnp.where(key == i, u_ref[i * 8 : i * 8 + 8, :], found)
        total = total + found * weight_ref[r : r + 1, :]
    bottom = total[0:4] + total[4:8]
    out_ref[width:, :] = jnp.concatenate(
        [bottom, jnp.zeros((out_ref.shape[0] - width - 4, col_max), F32)], axis=0
    ).astype(BF16)


def combine(layers, reaction_ref, all_ref, state_ref, bottom_ref):
    parts, rows, col_max = all_ref.shape
    out_species, species = reaction_ref.shape
    own = species // parts
    wide = own * layers
    width = out_species * layers
    mix = reaction_ref[...].astype(BF16)
    left = jnp.where(
        row_ids(width, out_species) // layers
        == lax.broadcasted_iota(jnp.int32, (width, out_species), 1),
        1.0,
        0.0,
    ).astype(BF16)
    right = jnp.where(
        row_ids(species, species * layers)
        == lax.broadcasted_iota(jnp.int32, (species, species * layers), 1) // layers,
        1.0,
        0.0,
    ).astype(BF16)
    full = nn(nn(left, mix).astype(BF16), right)
    same = (
        row_ids(width, species * layers) % layers
        == lax.broadcasted_iota(jnp.int32, (width, species * layers), 1) % layers
    )
    full = jnp.where(same, full, 0.0).astype(BF16)
    mixed = jnp.zeros((width, col_max), F32)
    bottom = jnp.zeros((out_species, col_max), F32)
    mix = mix.astype(F32)
    for k in range(parts):
        mixed = mixed + nn(full[:, k * wide : (k + 1) * wide], all_ref[k, :wide, :])
        tail = all_ref[k, wide:, :].astype(F32)
        for s in range(own):
            col = k * own + s
            bottom = bottom + mix[:, col : col + 1] * tail[s : s + 1, :]
    state_ref[...] = mixed.T.astype(BF16)
    bottom_ref[...] = bottom


def body(
    grad_columns,
    grad_flux,
    remap_part,
    remap_slot,
    remap_weight,
    col_count,
    neighbors,
    kappa,
    thickness,
    vertical,
    reaction,
):
    tiles = lax.axis_size("tile")
    parts = lax.axis_size("spec")
    col_max, width = grad_columns.shape
    layers = thickness.shape[1]
    part_t, slot_t, weight_t, nbr_t = remap_part.T, remap_slot.T, remap_weight.T, neighbors.T
    shape = jax.ShapeDtypeStruct
    payload, w, tv = call(
        prepare,
        [shape((ROWS, col_max), BF16), shape((width, col_max), F32), shape((width, 1), F32)],
        [SMEM] + [VMEM] * 8,
        flops=4 * 10**7,
        moved=10**6,
    )(col_count, grad_columns, vertical, thickness, grad_flux, part_t, slot_t, weight_t, nbr_t)
    data = lax.all_gather(payload, "tile", axis=0, tiled=True)
    rim = shape((width, LANES), BF16)
    counts, x, to_prev, to_next = call(
        first_step,
        [shape((col_max + 2 * LANES, col_max), BF16), shape((width, col_max), F32), rim, rim],
        [SMEM] + [VMEM] * 2,
        flops=10**9,
        moved=4 * 10**6,
    )(kappa, nbr_t, w)
    for step in range(1, SUB):
        from_next = shifted(to_prev, "tile", -1)
        from_prev = shifted(to_next, "tile", 1)
        x, to_prev, to_next = call(
            next_step,
            [shape((width, col_max), F32), rim, rim],
            [SMEM] + [VMEM] * 4,
            flops=4 * 10**8,
            moved=4 * 10**6,
        )(kappa, counts, x, from_prev, from_next)
    from_next = shifted(to_prev, "tile", -1)
    from_prev = shifted(to_next, "tile", 1)
    state = call(
        functools.partial(chain, tiles),
        [shape((tiles, 8, col_max), F32)],
        [SMEM] + [VMEM] * 2,
        scratch=[
            pltpu.VMEM((2, tiles, 8, col_max), F32),
            pltpu.VMEM((tiles * col_max // WIDE * 4, WIDE), F32),
        ],
        flops=10**10,
        moved=10**6,
    )(kappa, tv, data)[0]
    tail = 16
    mine = call(
        functools.partial(finish, tiles),
        [shape((width + tail, col_max), BF16)],
        [VMEM] * 8,
        scratch=[
            pltpu.VMEM((tiles * col_max // WIDE * 4, WIDE), F32),
            pltpu.VMEM((tiles * col_max // WIDE * 4, col_max), F32),
        ],
        flops=10**9,
        moved=10**6,
    )(x, from_prev, from_next, tv, state, part_t, slot_t, weight_t)[0]
    every = lax.all_gather(mine, "spec", axis=0, tiled=False)
    grad_state, grad_bottom = call(
        functools.partial(combine, layers),
        [shape((col_max, width), BF16), shape((reaction.shape[1], col_max), F32)],
        [VMEM] * 2,
        flops=2 * 10**8,
        moved=2 * 10**6,
    )(reaction.T, every)
    return grad_state, grad_bottom


def solution(mesh):
    placed = (
        P("tile", "spec"),
        P("spec", "tile"),
        P("tile", None),
        P("tile", None),
        P("tile", None),
        P("tile"),
        P("tile", None),
        P("spec"),
        P("spec", None),
        P("spec", None, None),
        P(None, "spec"),
    )
    return jax.shard_map(
        body,
        mesh=mesh,
        in_specs=placed,
        out_specs=(P("tile", "spec"), P("spec", "tile")),
        check_vma=False,
    )
```

profile of v0, /device:TPU:0, one launch (start us, length us, event | category | flops | bytes accessed | tf_op | source)
XLA Modules:
  0.0 139.6 jit_solution(6980403033265727297)
XLA Ops:
  7.9 0.9 copy-done.1
  8.8 0.8 copy-done.2
  9.6 0.7 copy-done.3
  13.8 0.8 shard_map.122
  16.0 3.6 %shard_map.123 = (bf16[1280,1024]{1,0:T(8,128)(2,1)S(1)}, f32[128,1024]{1,0:T(8,128)S(1)}, bf16[128,128]{1,0:T(8,128)(2,1)S(1)}, bf16[128,128]{1,0:T(8,128)(2,1)S(1)}) custom-call(f32[4]{0:T(128)S(1)} %copy-done.12, s32[4,1024]{1,0:T(4,128)S(1)} %bitcast.8, f32[128,1024]{1,0:T(8,128)S(1)} %get-tuple-element.18.w_ref), custom_call_target="tpu_custom_call" | custom-call | flops 1000000000 | bytes 4000000 | tf_op jit(solution)/shard_map/pallas_call | solution.py:325
  19.6 4.9 %collective-permute-start = (bf16[128,128]{1,0:T(8,128)(2,1)S(1)}, bf16[128,128]{1,0:T(8,128)(2,1)S(1)}, u32[]{:S(2)}, u32[]{:S(2)}) collective-permute-start(bf16[128,128]{1,0:T(8,128)(2,1)S(1)} %get-tuple-element.21), channel_id=1, source_target_pairs={{0,4},{4,8},{8,12},{12,16},{16,20},{20,24},{24,28},{1,5},{5,9},{9,... | collective-permute-start | bytes 98312 | tf_op jit(solution)/shard_map/ppermute | solution.py:24
  24.5 1.3 collective-permute-start.1
  26.1 4.2 %collective-permute-done.1.from_next = bf16[128,128]{1,0:T(8,128)(2,1)S(1)} collective-permute-done((bf16[128,128]{1,0:T(8,128)(2,1)S(1)}, bf16[128,128]{1,0:T(8,128)(2,1)S(1)}, u32[]{:S(2)}, u32[]{:S(2)}) %collective-permute-start.1) | collective-permute-done | bytes 32800 | tf_op jit(solution)/shard_map/ppermute | solution.py:24
  30.3 1.5 %shard_map.124 = (f32[128,1024]{1,0:T(8,128)S(1)}, bf16[128,128]{1,0:T(8,128)(2,1)S(1)}, bf16[128,128]{1,0:T(8,128)(2,1)S(1)}) custom-call(f32[4]{0:T(128)S(1)} %copy-done.12, bf16[1280,1024]{1,0:T(8,128)(2,1)S(1)} %get-tuple-element.19.counts_ref, f32[128,1024]{1,0:T(8,128)S(1)} %get-tuple-element.20.part_ref, ...), custom_call_target="tpu_custom_call" | custom-call | flops 400000000 | bytes 4000000 | tf_op jit(solution)/shard_map/pallas_call | solution.py:335
  31.9 4.3 %collective-permute-start.2 = (bf16[128,128]{1,0:T(8,128)(2,1)S(1)}, bf16[128,128]{1,0:T(8,128)(2,1)S(1)}, u32[]{:S(2)}, u32[]{:S(2)}) collective-permute-start(bf16[128,128]{1,0:T(8,128)(2,1)S(1)} %get-tuple-element.24), channel_id=1, source_target_pairs={{0,4},{4,8},{8,12},{12,16},{16,20},{20,24},{24,28},{1,5},{5,9},{9,... | collective-permute-start | bytes 98312 | tf_op jit(solution)/shard_map/ppermute | solution.py:24
  36.2 1.3 collective-permute-start.3
  37.8 4.2 %collective-permute-done.3.from_next = bf16[128,128]{1,0:T(8,128)(2,1)S(1)} collective-permute-done((bf16[128,128]{1,0:T(8,128)(2,1)S(1)}, bf16[128,128]{1,0:T(8,128)(2,1)S(1)}, u32[]{:S(2)}, u32[]{:S(2)}) %collective-permute-start.3) | collective-permute-done | bytes 32800 | tf_op jit(solution)/shard_map/ppermute | solution.py:24
  42.0 1.5 %shard_map.125 = (f32[128,1024]{1,0:T(8,128)S(1)}, bf16[128,128]{1,0:T(8,128)(2,1)S(1)}, bf16[128,128]{1,0:T(8,128)(2,1)S(1)}) custom-call(f32[4]{0:T(128)S(1)} %copy-done.12, bf16[1280,1024]{1,0:T(8,128)(2,1)S(1)} %get-tuple-element.19.counts_ref, f32[128,1024]{1,0:T(8,128)S(1)} %get-tuple-element.23.part_ref, ...), custom_call_target="tpu_custom_call" | custom-call | flops 400000000 | bytes 4000000 | tf_op jit(solution)/shard_map/pallas_call | solution.py:335
  43.5 3.4 %collective-permute-start.4 = (bf16[128,128]{1,0:T(8,128)(2,1)S(1)}, bf16[128,128]{1,0:T(8,128)(2,1)S(1)}, u32[]{:S(2)}, u32[]{:S(2)}) collective-permute-start(bf16[128,128]{1,0:T(8,128)(2,1)S(1)} %get-tuple-element.27), channel_id=1, source_target_pairs={{0,4},{4,8},{8,12},{12,16},{16,20},{20,24},{24,28},{1,5},{5,9},{9,... | collective-permute-start | bytes 98312 | tf_op jit(solution)/shard_map/ppermute | solution.py:24
  47.0 1.3 collective-permute-start.5
  48.3 32.2 %all_gather.9.data_ref = bf16[256,1024]{1,0:T(8,128)(2,1)S(1)} all-gather(bf16[32,1024]{1,0:T(8,128)(2,1)S(1)} %get-tuple-element.33), channel_id=1, replica_groups=mesh['tile'=8,'spec'=4] {'tile'}, dimensions={0}, use_global_device_ids=true | all-gather | bytes 589824 | tf_op jit(solution)/shard_map/all_gather | solution.py:323
  80.4 1.5 %shard_map.126 = (f32[128,1024]{1,0:T(8,128)S(1)}, bf16[128,128]{1,0:T(8,128)(2,1)S(1)}, bf16[128,128]{1,0:T(8,128)(2,1)S(1)}) custom-call(f32[4]{0:T(128)S(1)} %copy-done.13, bf16[1280,1024]{1,0:T(8,128)(2,1)S(1)} %get-tuple-element.19.counts_ref, f32[128,1024]{1,0:T(8,128)S(1)} %get-tuple-element.26.part_ref, ...), custom_call_target="tpu_custom_call" | custom-call | flops 400000000 | bytes 4000000 | tf_op jit(solution)/shard_map/pallas_call | solution.py:335
  82.0 1.6 %collective-permute-start.6 = (bf16[128,128]{1,0:T(8,128)(2,1)S(1)}, bf16[128,128]{1,0:T(8,128)(2,1)S(1)}, u32[]{:S(2)}, u32[]{:S(2)}) collective-permute-start(bf16[128,128]{1,0:T(8,128)(2,1)S(1)} %get-tuple-element.30), channel_id=1, source_target_pairs={{0,4},{4,8},{8,12},{12,16},{16,20},{20,24},{24,28},{1,5},{5,9},{9,... | collective-permute-start | bytes 98312 | tf_op jit(solution)/shard_map/ppermute | solution.py:24
  83.6 1.3 collective-permute-start.7
  85.0 24.0 %shard_map.127.chain_ref = f32[8,8,1024]{2,1,0:T(8,128)S(1)} custom-call(f32[4]{0:T(128)S(1)} %copy-done.13, f32[128,1]{1,0:T(8,128)S(1)} %get-tuple-element.32.tv_ref, bf16[256,1024]{1,0:T(8,128)(2,1)S(1)} %all_gather.9.data_ref), custom_call_target="tpu_custom_call" | custom-call | flops 10000000000 | bytes 1000000 | tf_op jit(solution)/shard_map/pallas_call | solution.py:344
  109.0 1.4 %shard_map.128 = bf16[144,1024]{1,0:T(8,128)(2,1)} custom-call(f32[128,1024]{1,0:T(8,128)S(1)} %get-tuple-element.29.part_ref, bf16[128,128]{1,0:T(8,128)(2,1)S(1)} %collective-permute-done.6.from_prev, bf16[128,128]{1,0:T(8,128)(2,1)S(1)} %collective-permute-done.7.from_next, f32[128,1]{1,0:T(8,128)S(1)} %get-tuple-element.32.tv_ref, ...), custom_call_target="tpu_custom_call" | custom-call | flops 1000000000 | bytes 1000000 | tf_op jit(solution)/shard_map/pallas_call | solution.py:356
  110.4 19.6 %all-gather.3.cloned.1.call-done = bf16[576,1024]{1,0:T(8,128)(2,1)} async-done(((bf16[144,1024]{1,0:T(8,128)(2,1)}), bf16[576,1024]{1,0:T(8,128)(2,1)}) %all-gather.3.cloned.1.call-update) | async-done | bytes 1179664 | tf_op jit(solution)/shard_map/all_gather | solution.py:367
  130.1 1.3 copy-done
  131.3 1.4 %shard_map.129 = (bf16[1024,128]{1,0:T(8,128)(2,1)}, f32[4,1024]{1,0:T(4,128)}) custom-call(bf16[4,16]{1,0:T(4,128)(2,1)S(1)} %bitcast.15, bf16[4,144,1024]{2,1,0:T(8,128)(2,1)S(1)} %bitcast.6), custom_call_target="tpu_custom_call" | custom-call | flops 200000000 | bytes 2000000 | tf_op jit(solution)/shard_map/pallas_call | solution.py:368
  (36 shorter events, 5.6 us)
Async XLA Ops:
  7.2 122.9 %all-gather.3.cloned.1.call-start = ((), (), s32[]{:S(2)}) async-start(), calls=%async_computation | async-start | bytes 1474560 | tf_op jit(solution)/shard_map/all_gather | solution.py:367
  7.9 1.0 copy-start.1
  8.8 0.8 copy-start.2
  9.6 0.7 copy-start.3
  10.3 0.7 copy-start.4
  11.0 0.7 copy-start.6
  11.7 0.7 copy-start.8
  12.4 0.7 copy-start.10
  13.2 0.7 copy-start.14
  14.6 0.7 copy-start.5
  19.6 6.5 %collective-permute-start = (bf16[128,128]{1,0:T(8,128)(2,1)S(1)}, bf16[128,128]{1,0:T(8,128)(2,1)S(1)}, u32[]{:S(2)}, u32[]{:S(2)}) collective-permute-start(bf16[128,128]{1,0:T(8,128)(2,1)S(1)} %get-tuple-element.21), channel_id=1, source_target_pairs={{0,4},{4,8},{8,12},{12,16},{16,20},{20,24},{24,28},{1,5},{5,9},{9,... | collective-permute-start | bytes 98312 | tf_op jit(solution)/shard_map/ppermute | solution.py:24
  24.5 5.8 %collective-permute-start.1 = (bf16[128,128]{1,0:T(8,128)(2,1)S(1)}, bf16[128,128]{1,0:T(8,128)(2,1)S(1)}, u32[]{:S(2)}, u32[]{:S(2)}) collective-permute-start(bf16[128,128]{1,0:T(8,128)(2,1)S(1)} %get-tuple-element.22), channel_id=1, source_target_pairs={{4,0},{8,4},{12,8},{16,12},{20,16},{24,20},{28,24},{5,1},{9,5},{13... | collective-permute-start | bytes 98312 | tf_op jit(solution)/shard_map/ppermute | solution.py:24
  31.8 48.6 %copy-start.13 = (f32[4]{0:T(128)S(1)}, f32[4]{0:T(128)}, u32[]{:S(2)}) copy-start(f32[4]{0:T(128)} %kappa_ref.9) | copy-start | bytes 52
  31.9 5.9 %collective-permute-start.2 = (bf16[128,128]{1,0:T(8,128)(2,1)S(1)}, bf16[128,128]{1,0:T(8,128)(2,1)S(1)}, u32[]{:S(2)}, u32[]{:S(2)}) collective-permute-start(bf16[128,128]{1,0:T(8,128)(2,1)S(1)} %get-tuple-element.24), channel_id=1, source_target_pairs={{0,4},{4,8},{8,12},{12,16},{16,20},{20,24},{24,28},{1,5},{5,9},{9,... | collective-permute-start | bytes 98312 | tf_op jit(solution)/shard_map/ppermute | solution.py:24
  36.2 5.8 %collective-permute-start.3 = (bf16[128,128]{1,0:T(8,128)(2,1)S(1)}, bf16[128,128]{1,0:T(8,128)(2,1)S(1)}, u32[]{:S(2)}, u32[]{:S(2)}) collective-permute-start(bf16[128,128]{1,0:T(8,128)(2,1)S(1)} %get-tuple-element.25), channel_id=1, source_target_pairs={{4,0},{8,4},{12,8},{16,12},{20,16},{24,20},{28,24},{5,1},{9,5},{13... | collective-permute-start | bytes 98312 | tf_op jit(solution)/shard_map/ppermute | solution.py:24
  43.5 36.9 %collective-permute-start.4 = (bf16[128,128]{1,0:T(8,128)(2,1)S(1)}, bf16[128,128]{1,0:T(8,128)(2,1)S(1)}, u32[]{:S(2)}, u32[]{:S(2)}) collective-permute-start(bf16[128,128]{1,0:T(8,128)(2,1)S(1)} %get-tuple-element.27), channel_id=1, source_target_pairs={{0,4},{4,8},{8,12},{12,16},{16,20},{20,24},{24,28},{1,5},{5,9},{9,... | collective-permute-start | bytes 98312 | tf_op jit(solution)/shard_map/ppermute | solution.py:24
  47.0 33.5 %collective-permute-start.5 = (bf16[128,128]{1,0:T(8,128)(2,1)S(1)}, bf16[128,128]{1,0:T(8,128)(2,1)S(1)}, u32[]{:S(2)}, u32[]{:S(2)}) collective-permute-start(bf16[128,128]{1,0:T(8,128)(2,1)S(1)} %get-tuple-element.28), channel_id=1, source_target_pairs={{4,0},{8,4},{12,8},{16,12},{20,16},{24,20},{28,24},{5,1},{9,5},{13... | collective-permute-start | bytes 98312 | tf_op jit(solution)/shard_map/ppermute | solution.py:24
  82.0 27.0 %collective-permute-start.6 = (bf16[128,128]{1,0:T(8,128)(2,1)S(1)}, bf16[128,128]{1,0:T(8,128)(2,1)S(1)}, u32[]{:S(2)}, u32[]{:S(2)}) collective-permute-start(bf16[128,128]{1,0:T(8,128)(2,1)S(1)} %get-tuple-element.30), channel_id=1, source_target_pairs={{0,4},{4,8},{8,12},{12,16},{16,20},{20,24},{24,28},{1,5},{5,9},{9,... | collective-permute-start | bytes 98312 | tf_op jit(solution)/shard_map/ppermute | solution.py:24
  83.6 25.3 %collective-permute-start.7 = (bf16[128,128]{1,0:T(8,128)(2,1)S(1)}, bf16[128,128]{1,0:T(8,128)(2,1)S(1)}, u32[]{:S(2)}, u32[]{:S(2)}) collective-permute-start(bf16[128,128]{1,0:T(8,128)(2,1)S(1)} %get-tuple-element.31), channel_id=1, source_target_pairs={{4,0},{8,4},{12,8},{16,12},{20,16},{24,20},{28,24},{5,1},{9,5},{13... | collective-permute-start | bytes 98312 | tf_op jit(solution)/shard_map/ppermute | solution.py:24
  84.9 24.0 %copy-start.7 = (s32[1024,4]{0,1:T(4,128)S(1)}, s32[1024,4]{0,1:T(4,128)}, u32[]{:S(2)}) copy-start(s32[1024,4]{0,1:T(4,128)} %param.13) | copy-start | bytes 49156
  84.9 24.0 %copy-start.9 = (s32[1024,4]{0,1:T(4,128)S(1)}, s32[1024,4]{0,1:T(4,128)}, u32[]{:S(2)}) copy-start(s32[1024,4]{0,1:T(4,128)} %param.14) | copy-start | bytes 49156
  84.9 24.0 %copy-start.11 = (f32[1024,4]{0,1:T(4,128)S(1)}, f32[1024,4]{0,1:T(4,128)}, u32[]{:S(2)}) copy-start(f32[1024,4]{0,1:T(4,128)} %param.15) | copy-start | bytes 49156
  108.9 21.1 %copy-start.15 = (bf16[16,4]{0,1:T(4,128)(2,1)S(1)}, bf16[16,4]{0,1:T(4,128)(2,1)}, u32[]{:S(2)}) copy-start(bf16[16,4]{0,1:T(4,128)(2,1)} %param.21) | copy-start | bytes 388
  130.1 1.3 copy-start
  (1 other events, 0.7 us)
Sparse Core Ops, SparseCore 0:
  110.5 19.4 all-gather.2
where the time goes:
time: 140 us
  Pallas kernels  35.7 us (26%)
  blocking collectives  32.2 us (23%)
  waiting for transfers between devices  28.7 us (20%)
  starting transfers between devices  19.5 us (14%)
  between operations  14.9 us (11%)
  local copies, waits for them, and re-layouts  8.64 us (6%)
    all_gather x1, blocking collectives, body(): data = lax.all_gather(payload, 'tile', axis=0, tiled=True)  32.2 us
    pallas_call x1, Pallas kernels, body(): call(functools.partial(chain, tiles), [shape((tiles, 8, col_max), F32)],...  24 us
    all_gather x1, waiting for transfers between devices, body(): every = lax.all_gather(mine, 'spec', axis=0, tiled=False)  19.6 us
    ppermute x8, starting transfers between devices, shifted(): return lax.ppermute(block, axis, route)  19.4 us
    ppermute x8, waiting for transfers between devices, shifted(): return lax.ppermute(block, axis, route)  9.03 us
    unnamed x32, local copies, waits for them, and re-layouts  8.64 us
    pallas_call x3, Pallas kernels, body(): call(next_step, [shape((width, col_max), F32), rim, rim], [SMEM] + [VMEM]...  4.55 us
    pallas_call x1, Pallas kernels, body(): call(first_step, [shape((col_max + 2 * LANES, col_max), BF16), shape((wid...  3.61 us
  transfers between devices with their start and end apart: 9, of which 5 were waited for; matrix products, arithmetic and copies ran while one was open for 0% of the time, Pallas kernels for 17%

commit v1 on v0

v1 whole, which is shorter than its diff:
```python
import functools

import jax
import jax.numpy as jnp
from jax import lax
from jax.experimental import pallas as pl
from jax.experimental.pallas import tpu as pltpu
from jax.sharding import PartitionSpec as P

SUB = 4
LANES = 128
WIDE = 256
OWN = 16
DEAD = 7
F32 = jnp.float32
BF16 = jnp.bfloat16
VMEM = pl.BlockSpec(memory_space=pltpu.VMEM)
ANY = pl.BlockSpec(memory_space=pl.ANY)
SMEM = pl.BlockSpec(memory_space=pltpu.SMEM)
LIMIT = 48 * 1024 * 1024


def call(kernel, outs, specs, scratch=(), flops=0, moved=0):
    return pl.pallas_call(
        kernel,
        out_shape=outs,
        in_specs=specs,
        out_specs=[VMEM] * len(outs),
        scratch_shapes=scratch,
        compiler_params=pltpu.CompilerParams(vmem_limit_bytes=LIMIT),
        cost_estimate=pl.CostEstimate(flops=flops, bytes_accessed=moved, transcendentals=0),
    )


def nt(a, b, precision=None):
    return lax.dot_general(
        a, b, (((1,), (1,)), ((), ())), precision=precision, preferred_element_type=F32
    )


def nn(a, b, precision=None):
    return lax.dot_general(
        a, b, (((1,), (0,)), ((), ())), precision=precision, preferred_element_type=F32
    )


def row_ids(rows, cols):
    return lax.broadcasted_iota(jnp.int32, (rows, cols), 0)


def fetch(pairs, sems):
    copies = [pltpu.make_async_copy(a, b, sems.at[i]) for i, (a, b) in enumerate(pairs)]
    for copy in copies:
        copy.start()
    for copy in copies:
        copy.wait()


def prepare(
    count_ref, gc_any, vert_any, thick_any, flux_any, part_any, slot_any, weight_any, nbr_any,
    payload_ref, tv_ref,
    gc_ref, vert_ref, thick_ref, flux_ref, part_ref, slot_ref, weight_ref, nbr_ref, sems,
):
    fetch(
        [
            (gc_any, gc_ref),
            (vert_any, vert_ref),
            (thick_any, thick_ref),
            (flux_any, flux_ref),
            (part_any, part_ref),
            (slot_any, slot_ref),
            (weight_any, weight_ref),
            (nbr_any, nbr_ref),
        ],
        sems,
    )
    tiles, block_rows, col_max = payload_ref.shape
    species, layers, _ = vert_ref.shape
    width = species * layers
    v = vert_ref[...].astype(F32).reshape(width, layers)
    v = jnp.concatenate([v] * species, axis=1)
    rows = row_ids(width, width) // layers
    cols = lax.broadcasted_iota(jnp.int32, (width, width), 1) // layers
    vt = jnp.where(rows == cols, v, 0.0).T
    hi = lax.Precision.HIGHEST
    v2 = nn(vt, vt, hi)
    v4 = nn(v2, v2, hi)
    th = jnp.concatenate([thick_ref[s : s + 1, :] for s in range(species)], axis=1)
    tv_ref[...] = nt(jnp.broadcast_to(th, (8, width)), v4, hi)
    live = lax.broadcasted_iota(jnp.int32, (1, col_max), 1) < count_ref[0]
    w = jnp.where(live, nt(v4.astype(BF16), gc_ref[...]), 0.0)
    top = [w[s * layers : s * layers + 1, :] for s in range(species)]
    slot, nbr = slot_ref[...], nbr_ref[...]
    power = (slot // WIDE) * 8 + jnp.where(live, nbr // WIDE, DEAD)
    code = 128.0 + part_ref[...].astype(F32)
    for bit in range(5):
        code = code * jnp.where((power >> bit) & 1 == 1, float(2 ** (2**bit)), 1.0)
    common = top + [
        flux_ref[...],
        weight_ref[...],
        (slot % WIDE).astype(F32),
        (nbr % WIDE).astype(F32),
        code,
    ]
    own = width // tiles
    pad = [] if own == OWN else [jnp.zeros((OWN - own, col_max), F32)]
    common = jnp.concatenate(common, axis=0).astype(BF16)
    for q in range(tiles):
        mine = jnp.concatenate([w[q * own : (q + 1) * own]] + pad, axis=0).astype(BF16)
        payload_ref[q] = jnp.concatenate([mine, common], axis=0)


def decoded(code):
    power = jnp.zeros(code.shape, jnp.int32)
    for bit in (16, 8, 4, 2, 1):
        large = code >= 128.0 * 2.0**bit
        code = jnp.where(large, code * 2.0**-bit, code)
        power = power + jnp.where(large, bit, 0)
    return code - 128.0, power


def hot(key, ids):
    return jnp.where(ids == key, jnp.ones((), BF16), jnp.zeros((), BF16))


def picked(keys, value, target):
    return jnp.where(keys == jnp.asarray(target, BF16), value, jnp.zeros((), BF16))


def chain(
    tiles, own, layers, keep, kappa_ref, tv_ref, data_ref, back_ref, y_ref, x_ref, table_ref, hot_ref
):
    col_max = data_ref.shape[2]
    subs = col_max // WIDE
    me = lax.axis_index("tile")
    ids = row_ids(WIDE, 1).astype(F32).astype(BF16)
    quarter = row_ids(16, 1) // 4

    table_ref[...] = jnp.zeros_like(table_ref)

    def gather(q, carry):
        block = data_ref[q].astype(F32)
        part, power = decoded(block[OWN + 20 : OWN + 24])
        sub = power >> 3
        for r in range(4):
            value = block[OWN + 4 : OWN + 8] * block[OWN + 8 + r : OWN + 9 + r]
            value = jnp.concatenate([value] * 4, axis=0).astype(BF16)
            key = jnp.where(sub[r : r + 1] == quarter, part[r : r + 1], -1.0).astype(BF16)
            rows = jnp.concatenate([picked(key, value, g) for g in range(tiles)], axis=0)
            low = block[OWN + 12 + r : OWN + 13 + r].astype(BF16)
            table_ref[...] += nt(rows, hot(low, ids))
        return carry

    lax.fori_loop(0, tiles, gather, 0)

    lane = lax.broadcasted_iota(jnp.int32, (OWN, tv_ref.shape[1]), 1)
    row = row_ids(OWN, 1)
    tv_own = jnp.sum(
        jnp.where((lane == me * own + row) & (row < own), tv_ref[0:1], 0.0), axis=1, keepdims=True
    )
    tv_top = jnp.sum(jnp.where(lane == row * layers, tv_ref[0:1], 0.0), axis=1, keepdims=True)[0:4]
    mine = me * own // layers
    for q in range(tiles):
        block = data_ref[q].astype(F32)
        live = decoded(block[OWN + 20 : OWN + 21])[1] & 7 != DEAD
        inj = [table_ref[q * 16 + h * 4 : q * 16 + h * 4 + 4, :] for h in range(subs)]
        inj = jnp.where(live, jnp.concatenate(inj, axis=1), 0.0)
        chosen_inj = jnp.zeros((1, col_max), F32)
        for s in range(4):
            chosen_inj = jnp.where(mine == s, inj[s : s + 1], chosen_inj)
        x_ref[0, q, 0:OWN] = block[0:OWN] + tv_own * chosen_inj
        x_ref[0, q, OWN : OWN + 4] = block[OWN : OWN + 4] + tv_top * inj

    k_own = kappa_ref[mine]
    k_top = jnp.zeros((4, 1), F32)
    for s in range(4):
        k_top = jnp.where(row_ids(4, 1) == s, kappa_ref[s], k_top)
    k_col = jnp.concatenate([jnp.full((OWN, 1), k_own, F32), k_top], axis=0)
    total_rows = OWN + 4

    for step in range(SUB):
        here, there = step % 2, (step + 1) % 2
        for q in range(tiles):
            x_ref[there, q] = (1.0 - 4.0 * k_col) * x_ref[here, q]

        def apply(q, carry):
            block = data_ref[q].astype(F32)
            power = decoded(block[OWN + 20 : OWN + 24])[1]
            high = power & 7
            value = k_col * x_ref[here, q]
            wide = value[0:OWN].astype(BF16)
            small = jnp.concatenate([value[OWN:total_rows]] * 4, axis=0).astype(BF16)
            total = jnp.zeros((7 * 16, WIDE), F32)
            for n in range(4):
                key = jnp.broadcast_to(high[n : n + 1].astype(F32), (16, col_max)).astype(BF16)
                skew = (high[n : n + 1] - quarter).astype(F32).astype(BF16)
                rows = [picked(key, wide, h) for h in range(5)]
                rows += [picked(skew, small, 0), picked(skew, small, 4)]
                rows = jnp.concatenate(rows, axis=0)
                low = block[OWN + 16 + n : OWN + 17 + n].astype(BF16)
                if not keep:
                    ones = hot(low, ids)
                elif step == 0:
                    ones = hot(low, ids)
                    hot_ref[q * 4 + n] = ones
                else:
                    ones = hot_ref[q * 4 + n]
                total = total + nt(rows, ones)
            for h in range(subs):
                cols = slice(h * WIDE, (h + 1) * WIDE)
                x_ref[there, q, 0:OWN, cols] += total[h * 16 : h * 16 + 16]
                x_ref[there, q, OWN:total_rows, cols] += total[80 + 4 * h : 84 + 4 * h]
            cross = jnp.concatenate([total[64:80], total[96:100]], axis=0)
            before, after = jnp.maximum(q - 1, 0), jnp.minimum(q + 1, tiles - 1)
            x_ref[there, before, :, LANES : 2 * LANES] += jnp.where(q > 0, cross[:, :LANES], 0.0)
            x_ref[there, after, :, :LANES] += jnp.where(q < tiles - 1, cross[:, LANES:], 0.0)
            return carry

        lax.fori_loop(0, tiles, apply, 0)
    for q in range(tiles):
        back_ref[q] = x_ref[SUB % 2, q, 0:own].astype(BF16)
        y_ref[q] = x_ref[SUB % 2, q, OWN:total_rows]


def gather_bottom(
    tiles, y_ref, part_any, slot_any, weight_any, out_ref, table_ref, found_ref,
    part_ref, slot_ref, weight_ref, sems,
):
    fetch([(part_any, part_ref), (slot_any, slot_ref), (weight_any, weight_ref)], sems)
    col_max = part_ref.shape[1]
    subs = col_max // WIDE
    half = tiles * subs // 2
    for i in range(half):
        first, other = i, i + half
        a = y_ref[first // subs, :, (first % subs) * WIDE : (first % subs + 1) * WIDE]
        b = y_ref[other // subs, :, (other % subs) * WIDE : (other % subs + 1) * WIDE]
        table_ref[i * 8 : i * 8 + 8, :] = jnp.concatenate([a, b], axis=0)
    table = table_ref[...].astype(BF16)
    slot = slot_ref[...]
    high = part_ref[...] * subs + slot // WIDE
    low = (slot % WIDE).astype(F32).astype(BF16)
    ids = row_ids(WIDE, 1).astype(F32).astype(BF16)
    offset = jnp.where(row_ids(8, 1) >= 4, half, 0)
    total = jnp.zeros((8, col_max), F32)
    for r in range(4):
        found_ref[...] = nn(table, hot(low[r : r + 1], ids))
        key = high[r : r + 1] - offset
        found = jnp.zeros((8, col_max), F32)
        for i in range(half):
            found = jnp.where(key == i, found_ref[i * 8 : i * 8 + 8, :], found)
        total = total + found * weight_ref[r : r + 1, :]
    bottom = total[0:4] + total[4:8]
    out_ref[...] = jnp.concatenate(
        [bottom, jnp.zeros((out_ref.shape[0] - 4, col_max), F32)], axis=0
    ).astype(BF16)


def combine(layers, reaction_ref, all_ref, tail_ref, state_ref, bottom_ref):
    parts, wide, col_max = all_ref.shape
    out_species, species = reaction_ref.shape
    own = species // parts
    width = out_species * layers
    mix = reaction_ref[...].astype(BF16)
    left = jnp.where(
        row_ids(width, out_species) // layers
        == lax.broadcasted_iota(jnp.int32, (width, out_species), 1),
        1.0,
        0.0,
    ).astype(BF16)
    right = jnp.where(
        row_ids(species, species * layers)
        == lax.broadcasted_iota(jnp.int32, (species, species * layers), 1) // layers,
        1.0,
        0.0,
    ).astype(BF16)
    full = nn(nn(left, mix).astype(BF16), right)
    same = (
        row_ids(width, species * layers) % layers
        == lax.broadcasted_iota(jnp.int32, (width, species * layers), 1) % layers
    )
    full = jnp.where(same, full, 0.0).astype(BF16)
    mixed = jnp.zeros((width, col_max), F32)
    bottom = jnp.zeros((out_species, col_max), F32)
    mix = mix.astype(F32)
    for k in range(parts):
        mixed = mixed + nn(full[:, k * wide : (k + 1) * wide], all_ref[k])
        tail = tail_ref[k].astype(F32)
        for s in range(own):
            col = k * own + s
            bottom = bottom + mix[:, col : col + 1] * tail[s : s + 1, :]
    state_ref[...] = mixed.T.astype(BF16)
    bottom_ref[...] = bottom


def body(
    grad_columns,
    grad_flux,
    remap_part,
    remap_slot,
    remap_weight,
    col_count,
    neighbors,
    kappa,
    thickness,
    vertical,
    reaction,
):
    tiles = lax.axis_size("tile")
    col_max, width = grad_columns.shape
    layers = thickness.shape[1]
    own = width // tiles
    entries = tiles * col_max // WIDE
    part_t, slot_t, weight_t, nbr_t = remap_part.T, remap_slot.T, remap_weight.T, neighbors.T
    shape = jax.ShapeDtypeStruct
    moved = [grad_columns, vertical, thickness, grad_flux, part_t, slot_t, weight_t, nbr_t]
    payload, tv = call(
        prepare,
        [shape((tiles, OWN + 24, col_max), BF16), shape((8, width), F32)],
        [SMEM] + [ANY] * 8,
        scratch=[pltpu.VMEM(a.shape, a.dtype) for a in moved] + [pltpu.SemaphoreType.DMA((8,))],
        flops=4 * 10**7,
        moved=10**6,
    )(col_count, *moved)
    data = lax.all_to_all(payload, "tile", split_axis=0, concat_axis=0, tiled=True)
    keep = tiles * 4 * WIDE * col_max * 2 <= 2**24
    back, y = call(
        functools.partial(chain, tiles, own, layers, keep),
        [shape((tiles, own, col_max), BF16), shape((tiles, 4, col_max), F32)],
        [SMEM] + [VMEM] * 2,
        scratch=[
            pltpu.VMEM((2, tiles, OWN + 4, col_max), F32),
            pltpu.VMEM((tiles * 16, WIDE), F32),
            pltpu.VMEM((tiles * 4 if keep else 1, WIDE, col_max), BF16),
        ],
        flops=10**10,
        moved=10**6,
    )(kappa, tv, data)
    home = lax.all_to_all(back, "tile", split_axis=0, concat_axis=0, tiled=True)
    remaps = [part_t, slot_t, weight_t]
    bottom = call(
        functools.partial(gather_bottom, tiles),
        [shape((16, col_max), BF16)],
        [VMEM] + [ANY] * 3,
        scratch=[pltpu.VMEM((entries * 4, WIDE), F32), pltpu.VMEM((entries * 4, col_max), F32)]
        + [pltpu.VMEM(a.shape, a.dtype) for a in remaps]
        + [pltpu.SemaphoreType.DMA((3,))],
        flops=10**9,
        moved=10**6,
    )(y, *remaps)[0]
    every_bottom = lax.all_gather(bottom, "spec", axis=0, tiled=False)
    every = lax.all_gather(home.reshape(width, col_max), "spec", axis=0, tiled=False)
    grad_state, grad_bottom = call(
        functools.partial(combine, layers),
        [shape((col_max, width), BF16), shape((reaction.shape[1], col_max), F32)],
        [VMEM] * 3,
        flops=2 * 10**8,
        moved=2 * 10**6,
    )(reaction.T, every, every_bottom)
    return grad_state, grad_bottom


def solution(mesh):
    placed = (
        P("tile", "spec"),
        P("spec", "tile"),
        P("tile", None),
        P("tile", None),
        P("tile", None),
        P("tile"),
        P("tile", None),
        P("spec"),
        P("spec", None),
        P("spec", None, None),
        P(None, "spec"),
    )
    return jax.shard_map(
        body,
        mesh=mesh,
        in_specs=placed,
        out_specs=(P("tile", "spec"), P("spec", "tile")),
        check_vma=False,
    )
```

time: 140 us -> 113 us (0.81)
  waiting for transfers between devices: 28.7 us -> 9.21 us
  starting transfers between devices: 19.5 us -> 0.04 us
  blocking collectives: 32.2 us -> 42.1 us
  Pallas kernels: 35.7 us -> 37.3 us
    all_to_all x0 -> x2, blocking collectives: none -> 36.7 us  [the longest x1 24.8 us: body(): lax.all_to_all(payload, 'tile', split_axis=0, concat_axis=0, tiled=True)]
    all_gather x1, blocking collectives: 32.2 us -> 5.43 us  [body(): every_bottom = lax.all_gather(bottom, 'spec', axis=0, tiled=False)]
    ppermute x8 -> x0, starting transfers between devices: 19.4 us -> none  [shifted(): return lax.ppermute(block, axis, route)]
    all_gather x1, waiting for transfers between devices: 19.6 us -> 9.2 us  [body(): lax.all_gather(home.reshape(width, col_max), 'spec', axis=0, tiled=False)]
    ppermute x8 -> x0, waiting for transfers between devices: 9.03 us -> none  [shifted(): return lax.ppermute(block, axis, route)]
    pallas_call x7 -> x3, Pallas kernels: 34.3 us -> 35.9 us  [the longest x1 34.2 us: body(): call(functools.partial(chain, tiles, own, layers, keep), [shape((tiles, o...]
    unnamed x32 -> x28, local copies, waits for them, and re-layouts: 8.64 us -> 9.25 us
  transfers between devices with their start and end apart: 9 -> 1, of which waited for: 5 -> 1; matrix products, arithmetic and copies ran while one was open for 0% -> 0% of each run, Pallas kernels for 17% -> 0%
where the time goes in v1:
time: 113 us
  blocking collectives  42.1 us (37%)
  Pallas kernels  37.3 us (33%)
  between operations  14.7 us (13%)
  local copies, waits for them, and re-layouts  9.25 us (8%)
  waiting for transfers between devices  9.21 us (8%)
    pallas_call x1, Pallas kernels, body(): call(functools.partial(chain, tiles, own, layers, keep), [shape((tiles, o...  34.2 us
    all_to_all x1, blocking collectives, body(): lax.all_to_all(payload, 'tile', split_axis=0, concat_axis=0, tiled=True)  24.8 us
    all_to_all x1, blocking collectives, body(): home = lax.all_to_all(back, 'tile', split_axis=0, concat_axis=0, tiled=True)  11.9 us
    unnamed x28, local copies, waits for them, and re-layouts  9.25 us
    all_gather x1, waiting for transfers between devices, body(): lax.all_gather(home.reshape(width, col_max), 'spec', axis=0, tiled=False)  9.2 us
    all_gather x1, blocking collectives, body(): every_bottom = lax.all_gather(bottom, 'spec', axis=0, tiled=False)  5.43 us
  transfers between devices with their start and end apart: 1, of which 1 were waited for; matrix products, arithmetic and copies ran while one was open for 0% of the time, Pallas kernels for 0%

profile of v1, /device:TPU:0, one launch (start us, length us, event | category | flops | bytes accessed | tf_op | source)
XLA Modules:
  0.0 112.6 jit_solution(17150528791075235800)
XLA Ops:
  7.2 0.0 all-gather.3.cloned.1.call-start
  7.9 0.7 copy-done.11
  8.5 0.9 copy-done.1
  9.5 0.8 copy-done.2
  10.2 0.7 copy-done.3
  11.0 0.7 copy-done.4
  11.7 0.7 copy-done.5
  12.4 0.7 copy-done.7
  13.1 0.7 copy-done.9
  13.8 1.2 %shard_map.122 = (bf16[8,40,1024]{2,1,0:T(8,128)(2,1)S(1)}, f32[8,128]{1,0:T(8,128)S(1)}) custom-call(s32[1]{0:T(128)S(6)} %copy.13.count_ref, bf16[1024,128]{1,0:T(8,128)(2,1)S(1)} %copy-done.1, bf16[4,32,32]{2,1,0:T(8,128)(2,1)S(1)} %copy-done.2, f32[4,32]{1,0:T(4,128)S(1)} %copy-done.11, f32[4,1024]{1,0:T(4,128)S(1)} %copy-done.3, s32[4,1024]{1,0:T(4,128)S(1)} %bitcast.9, ...), custom_call_target="tpu_custom_call" | custom-call | flops 40000000 | bytes 1000000 | tf_op jit(solution)/shard_map/pallas_call | solution.py:316
  15.0 24.8 %all_to_all.10.data_ref = bf16[8,40,1024]{2,1,0:T(8,128)(2,1)S(1)} all-to-all(bf16[8,40,1024]{2,1,0:T(8,128)(2,1)S(1)} %get-tuple-element.7), channel_id=1, replica_groups=mesh['tile'=8,'spec'=4] {'tile'}, dimensions={0} | all-to-all | bytes 1310720 | tf_op jit(solution)/shard_map/all_to_all | solution.py:324
  39.8 0.7 copy-done.13
  40.5 34.2 %shard_map.123 = (bf16[8,16,1024]{2,1,0:T(8,128)(2,1)S(1)}, f32[8,4,1024]{2,1,0:T(4,128)S(1)}) custom-call(f32[4]{0:T(128)S(1)} %copy-done.13, f32[8,128]{1,0:T(8,128)S(1)} %get-tuple-element.6.tv_ref, bf16[8,40,1024]{2,1,0:T(8,128)(2,1)S(1)} %all_to_all.10.data_ref), custom_call_target="tpu_custom_call" | custom-call | flops 10000000000 | bytes 1000000 | tf_op jit(solution)/shard_map/pallas_call | solution.py:326
  74.7 11.9 %all_to_all.11 = bf16[8,16,1024]{2,1,0:T(8,128)(2,1)} all-to-all(bf16[8,16,1024]{2,1,0:T(8,128)(2,1)S(1)} %get-tuple-element.8), channel_id=1, replica_groups=mesh['tile'=8,'spec'=4] {'tile'}, dimensions={0} | all-to-all | bytes 524288 | tf_op jit(solution)/shard_map/all_to_all | solution.py:338
  86.5 0.0 all-gather.3.cloned.1.call-update
  86.6 0.7 copy-done.6
  87.3 0.0 copy-done.8
  87.3 0.0 copy-done.10
  87.3 0.5 shard_map.124
  87.8 5.4 %all-gather = bf16[64,1024]{1,0:T(8,128)(2,1)S(1)} all-gather(bf16[16,1024]{1,0:T(8,128)(2,1)S(1)} %shard_map.124), channel_id=2, replica_groups=mesh['tile'=8,'spec'=4] {'spec'}, dimensions={0}, use_global_device_ids=true | all-gather | bytes 163840 | tf_op jit(solution)/shard_map/all_gather | solution.py:350
  93.3 9.2 %all-gather.3.cloned.1.call-done.all_ref = bf16[4,128,1024]{2,1,0:T(8,128)(2,1)} async-done(((bf16[1,128,1024]{2,1,0:T(8,128)(2,1)}), bf16[4,128,1024]{2,1,0:T(8,128)(2,1)}) %all-gather.3.cloned.1.call-update) | async-done | bytes 1048592 | tf_op jit(solution)/shard_map/all_gather | solution.py:351
  102.5 0.7 copy-done.12
  103.1 1.2 %copy-done = bf16[4,128,1024]{2,1,0:T(8,128)(2,1)S(1)} copy-done((bf16[4,128,1024]{2,1,0:T(8,128)(2,1)S(1)}, bf16[4,128,1024]{2,1,0:T(8,128)(2,1)}, u32[]{:S(2)}) %copy-start) | copy-done | bytes 1048600
  104.4 1.4 %shard_map.125 = (bf16[1024,128]{1,0:T(8,128)(2,1)}, f32[4,1024]{1,0:T(4,128)}) custom-call(bf16[4,16]{1,0:T(4,128)(2,1)S(1)} %bitcast.15, bf16[4,128,1024]{2,1,0:T(8,128)(2,1)S(1)} %copy-done, bf16[4,16,1024]{2,1,0:T(8,128)(2,1)S(1)} %bitcast.7), custom_call_target="tpu_custom_call" | custom-call | flops 200000000 | bytes 2000000 | tf_op jit(solution)/shard_map/pallas_call | solution.py:352
  (14 shorter events, 0.0 us)
Async XLA Ops:
  7.2 95.3 %all-gather.3.cloned.1.call-start = ((), (), s32[]{:S(2)}) async-start(), calls=%async_computation.2 | async-start | bytes 1310720 | tf_op jit(solution)/shard_map/all_gather | solution.py:351
  7.9 0.7 copy-start.11
  8.5 0.9 copy-start.1
  9.5 0.8 copy-start.2
  10.2 0.7 copy-start.3
  11.0 0.7 copy-start.4
  11.7 0.7 copy-start.5
  12.4 0.7 copy-start.7
  13.1 0.7 copy-start.9
  39.8 0.7 copy-start.13
  86.5 0.7 copy-start.6
  86.5 0.7 copy-start.8
  86.5 0.7 copy-start.10
  102.5 0.7 copy-start.12
  103.1 1.2 %copy-start = (bf16[4,128,1024]{2,1,0:T(8,128)(2,1)S(1)}, bf16[4,128,1024]{2,1,0:T(8,128)(2,1)}, u32[]{:S(2)}) copy-start(bf16[4,128,1024]{2,1,0:T(8,128)(2,1)} %all-gather.3.cloned.1.call-done.all_ref) | copy-start | bytes 3145732
Sparse Core Ops, SparseCore 0:
  86.7 15.7 all-gather.2

commit v2 on v1

--- a/solution.py
+++ b/solution.py
@@ -15,7 +15,7 @@
 F32 = jnp.float32
 BF16 = jnp.bfloat16
 VMEM = pl.BlockSpec(memory_space=pltpu.VMEM)
-ANY = pl.BlockSpec(memory_space=pl.ANY)
+HBM = pl.BlockSpec(memory_space=pltpu.HBM)
 SMEM = pl.BlockSpec(memory_space=pltpu.SMEM)
 LIMIT = 48 * 1024 * 1024
 
@@ -148,7 +148,7 @@
             key = jnp.where(sub[r : r + 1] == quarter, part[r : r + 1], -1.0).astype(BF16)
             rows = jnp.concatenate([picked(key, value, g) for g in range(tiles)], axis=0)
             low = block[OWN + 12 + r : OWN + 13 + r].astype(BF16)
-            table_ref[...] += nt(rows, hot(low, ids))
+            table_ref[...] += nt(hot(low, ids), rows)
         return carry
 
     lax.fori_loop(0, tiles, gather, 0)
@@ -160,10 +160,11 @@
     )
     tv_top = jnp.sum(jnp.where(lane == row * layers, tv_ref[0:1], 0.0), axis=1, keepdims=True)[0:4]
     mine = me * own // layers
+    table = table_ref[...].T
     for q in range(tiles):
         block = data_ref[q].astype(F32)
         live = decoded(block[OWN + 20 : OWN + 21])[1] & 7 != DEAD
-        inj = [table_ref[q * 16 + h * 4 : q * 16 + h * 4 + 4, :] for h in range(subs)]
+        inj = [table[q * 16 + h * 4 : q * 16 + h * 4 + 4, :] for h in range(subs)]
         inj = jnp.where(live, jnp.concatenate(inj, axis=1), 0.0)
         chosen_inj = jnp.zeros((1, col_max), F32)
         for s in range(4):
@@ -190,12 +191,12 @@
             value = k_col * x_ref[here, q]
             wide = value[0:OWN].astype(BF16)
             small = jnp.concatenate([value[OWN:total_rows]] * 4, axis=0).astype(BF16)
-            total = jnp.zeros((7 * 16, WIDE), F32)
+            total = jnp.zeros((WIDE, 8 * 16), F32)
             for n in range(4):
                 key = jnp.broadcast_to(high[n : n + 1].astype(F32), (16, col_max)).astype(BF16)
                 skew = (high[n : n + 1] - quarter).astype(F32).astype(BF16)
                 rows = [picked(key, wide, h) for h in range(5)]
-                rows += [picked(skew, small, 0), picked(skew, small, 4)]
+                rows += [picked(skew, small, 0), picked(skew, small, 4), jnp.zeros((16, col_max), BF16)]
                 rows = jnp.concatenate(rows, axis=0)
                 low = block[OWN + 16 + n : OWN + 17 + n].astype(BF16)
                 if not keep:
@@ -205,7 +206,8 @@
                     hot_ref[q * 4 + n] = ones
                 else:
                     ones = hot_ref[q * 4 + n]
-                total = total + nt(rows, ones)
+                total = total + nt(ones, rows)
+            total = total.T
             for h in range(subs):
                 cols = slice(h * WIDE, (h + 1) * WIDE)
                 x_ref[there, q, 0:OWN, cols] += total[h * 16 : h * 16 + 16]
@@ -316,7 +318,7 @@
     payload, tv = call(
         prepare,
         [shape((tiles, OWN + 24, col_max), BF16), shape((8, width), F32)],
-        [SMEM] + [ANY] * 8,
+        [SMEM] + [HBM] * 8,
         scratch=[pltpu.VMEM(a.shape, a.dtype) for a in moved] + [pltpu.SemaphoreType.DMA((8,))],
         flops=4 * 10**7,
         moved=10**6,
@@ -329,7 +331,7 @@
         [SMEM] + [VMEM] * 2,
         scratch=[
             pltpu.VMEM((2, tiles, OWN + 4, col_max), F32),
-            pltpu.VMEM((tiles * 16, WIDE), F32),
+            pltpu.VMEM((WIDE, tiles * 16), F32),
             pltpu.VMEM((tiles * 4 if keep else 1, WIDE, col_max), BF16),
         ],
         flops=10**10,
@@ -340,7 +342,7 @@
     bottom = call(
         functools.partial(gather_bottom, tiles),
         [shape((16, col_max), BF16)],
-        [VMEM] + [ANY] * 3,
+        [VMEM] + [HBM] * 3,
         scratch=[pltpu.VMEM((entries * 4, WIDE), F32), pltpu.VMEM((entries * 4, col_max), F32)]
         + [pltpu.VMEM(a.shape, a.dtype) for a in remaps]
         + [pltpu.SemaphoreType.DMA((3,))],

time: 113 us -> 114 us (level)
  no operation moved by 1% of the time
where the time goes in v2:
time: 114 us; the launch traced here: 113 us
  blocking collectives  42.1 us (37%)
  Pallas kernels  37.5 us (33%)
  between operations  14.7 us (13%)
  local copies, waits for them, and re-layouts  9.25 us (8%)
  waiting for transfers between devices  9.22 us (8%)
    pallas_call x1, Pallas kernels, body(): call(functools.partial(chain, tiles, own, layers, keep), [shape((tiles, o...  34.4 us
    all_to_all x1, blocking collectives, body(): lax.all_to_all(payload, 'tile', split_axis=0, concat_axis=0, tiled=True)  24.8 us
    all_to_all x1, blocking collectives, body(): home = lax.all_to_all(back, 'tile', split_axis=0, concat_axis=0, tiled=True)  11.9 us
    unnamed x28, local copies, waits for them, and re-layouts  9.25 us
    all_gather x1, waiting for transfers between devices, body(): lax.all_gather(home.reshape(width, col_max), 'spec', axis=0, tiled=False)  9.2 us
    all_gather x1, blocking collectives, body(): every_bottom = lax.all_gather(bottom, 'spec', axis=0, tiled=False)  5.43 us
  transfers between devices with their start and end apart: 1, of which 1 were waited for; matrix products, arithmetic and copies ran while one was open for 0% of the time, Pallas kernels for 0%

profile of v2, /device:TPU:0, one launch (start us, length us, event | category | flops | bytes accessed | tf_op | source)
XLA Modules:
  0.0 112.8 jit_solution(6256623109310072288)
XLA Ops:
  7.2 0.0 all-gather.3.cloned.1.call-start
  7.9 0.7 copy-done.11
  8.5 0.9 copy-done.1
  9.5 0.8 copy-done.2
  10.2 0.7 copy-done.3
  11.0 0.7 copy-done.4
  11.7 0.7 copy-done.5
  12.4 0.7 copy-done.7
  13.1 0.7 copy-done.9
  13.8 1.2 %shard_map.122 = (bf16[8,40,1024]{2,1,0:T(8,128)(2,1)S(1)}, f32[8,128]{1,0:T(8,128)S(1)}) custom-call(s32[1]{0:T(128)S(6)} %copy.13.count_ref, bf16[1024,128]{1,0:T(8,128)(2,1)S(1)} %copy-done.1, bf16[4,32,32]{2,1,0:T(8,128)(2,1)S(1)} %copy-done.2, f32[4,32]{1,0:T(4,128)S(1)} %copy-done.11, f32[4,1024]{1,0:T(4,128)S(1)} %copy-done.3, s32[4,1024]{1,0:T(4,128)S(1)} %bitcast.9, ...), custom_call_target="tpu_custom_call" | custom-call | flops 40000000 | bytes 1000000 | tf_op jit(solution)/shard_map/pallas_call | solution.py:318
  15.0 24.8 %all_to_all.10.data_ref = bf16[8,40,1024]{2,1,0:T(8,128)(2,1)S(1)} all-to-all(bf16[8,40,1024]{2,1,0:T(8,128)(2,1)S(1)} %get-tuple-element.7), channel_id=1, replica_groups=mesh['tile'=8,'spec'=4] {'tile'}, dimensions={0} | all-to-all | bytes 1310720 | tf_op jit(solution)/shard_map/all_to_all | solution.py:326
  39.8 0.7 copy-done.13
  40.5 34.4 %shard_map.123 = (bf16[8,16,1024]{2,1,0:T(8,128)(2,1)S(1)}, f32[8,4,1024]{2,1,0:T(4,128)S(1)}) custom-call(f32[4]{0:T(128)S(1)} %copy-done.13, f32[8,128]{1,0:T(8,128)S(1)} %get-tuple-element.6.tv_ref, bf16[8,40,1024]{2,1,0:T(8,128)(2,1)S(1)} %all_to_all.10.data_ref), custom_call_target="tpu_custom_call" | custom-call | flops 10000000000 | bytes 1000000 | tf_op jit(solution)/shard_map/pallas_call | solution.py:328
  74.9 11.9 %all_to_all.11 = bf16[8,16,1024]{2,1,0:T(8,128)(2,1)} all-to-all(bf16[8,16,1024]{2,1,0:T(8,128)(2,1)S(1)} %get-tuple-element.8), channel_id=1, replica_groups=mesh['tile'=8,'spec'=4] {'tile'}, dimensions={0} | all-to-all | bytes 524288 | tf_op jit(solution)/shard_map/all_to_all | solution.py:340
  86.8 0.0 all-gather.3.cloned.1.call-update
  86.8 0.7 copy-done.6
  87.5 0.0 copy-done.8
  87.5 0.0 copy-done.10
  87.5 0.5 shard_map.124
  88.0 5.4 %all-gather = bf16[64,1024]{1,0:T(8,128)(2,1)S(1)} all-gather(bf16[16,1024]{1,0:T(8,128)(2,1)S(1)} %shard_map.124), channel_id=2, replica_groups=mesh['tile'=8,'spec'=4] {'spec'}, dimensions={0}, use_global_device_ids=true | all-gather | bytes 163840 | tf_op jit(solution)/shard_map/all_gather | solution.py:352
  93.5 9.2 %all-gather.3.cloned.1.call-done.all_ref = bf16[4,128,1024]{2,1,0:T(8,128)(2,1)} async-done(((bf16[1,128,1024]{2,1,0:T(8,128)(2,1)}), bf16[4,128,1024]{2,1,0:T(8,128)(2,1)}) %all-gather.3.cloned.1.call-update) | async-done | bytes 1048592 | tf_op jit(solution)/shard_map/all_gather | solution.py:353
  102.7 0.7 copy-done.12
  103.4 1.2 %copy-done = bf16[4,128,1024]{2,1,0:T(8,128)(2,1)S(1)} copy-done((bf16[4,128,1024]{2,1,0:T(8,128)(2,1)S(1)}, bf16[4,128,1024]{2,1,0:T(8,128)(2,1)}, u32[]{:S(2)}) %copy-start) | copy-done | bytes 1048600
  104.6 1.4 %shard_map.125 = (bf16[1024,128]{1,0:T(8,128)(2,1)}, f32[4,1024]{1,0:T(4,128)}) custom-call(bf16[4,16]{1,0:T(4,128)(2,1)S(1)} %bitcast.15, bf16[4,128,1024]{2,1,0:T(8,128)(2,1)S(1)} %copy-done, bf16[4,16,1024]{2,1,0:T(8,128)(2,1)S(1)} %bitcast.7), custom_call_target="tpu_custom_call" | custom-call | flops 200000000 | bytes 2000000 | tf_op jit(solution)/shard_map/pallas_call | solution.py:354
  (14 shorter events, 0.0 us)
Async XLA Ops:
  7.2 95.5 %all-gather.3.cloned.1.call-start = ((), (), s32[]{:S(2)}) async-start(), calls=%async_computation.2 | async-start | bytes 1310720 | tf_op jit(solution)/shard_map/all_gather | solution.py:353
  7.9 0.7 copy-start.11
  8.5 0.9 copy-start.1
  9.5 0.8 copy-start.2
  10.2 0.7 copy-start.3
  11.0 0.7 copy-start.4
  11.7 0.7 copy-start.5
  12.4 0.7 copy-start.7
  13.1 0.7 copy-start.9
  39.8 0.7 copy-start.13
  86.7 0.7 copy-start.6
  86.7 0.7 copy-start.8
  86.7 0.7 copy-start.10
  102.7 0.7 copy-start.12
  103.4 1.2 %copy-start = (bf16[4,128,1024]{2,1,0:T(8,128)(2,1)S(1)}, bf16[4,128,1024]{2,1,0:T(8,128)(2,1)}, u32[]{:S(2)}) copy-start(bf16[4,128,1024]{2,1,0:T(8,128)(2,1)} %all-gather.3.cloned.1.call-done.all_ref) | copy-start | bytes 3145732
Sparse Core Ops, SparseCore 0:
  86.9 15.7 all-gather.2

commit v3 on v2

v3 whole, which is shorter than its diff:
```python
import functools

import jax
import jax.numpy as jnp
from jax import lax
from jax.experimental import pallas as pl
from jax.experimental.pallas import tpu as pltpu
from jax.sharding import PartitionSpec as P

SUB = 4
LANES = 128
WIDE = 256
OWN = 16
DEAD = 7
F32 = jnp.float32
BF16 = jnp.bfloat16
VMEM = pl.BlockSpec(memory_space=pltpu.VMEM)
HBM = pl.BlockSpec(memory_space=pltpu.HBM)
SMEM = pl.BlockSpec(memory_space=pltpu.SMEM)
LIMIT = 40 * 1024 * 1024
MOST = 60 * 1024 * 1024


def call(kernel, outs, specs, scratch=(), flops=0, moved=0, limit=LIMIT):
    return pl.pallas_call(
        kernel,
        out_shape=outs,
        in_specs=specs,
        out_specs=[VMEM] * len(outs),
        scratch_shapes=scratch,
        compiler_params=pltpu.CompilerParams(vmem_limit_bytes=limit),
        cost_estimate=pl.CostEstimate(flops=flops, bytes_accessed=moved, transcendentals=0),
    )


def nt(a, b, precision=None):
    return lax.dot_general(
        a, b, (((1,), (1,)), ((), ())), precision=precision, preferred_element_type=F32
    )


def nn(a, b, precision=None):
    return lax.dot_general(
        a, b, (((1,), (0,)), ((), ())), precision=precision, preferred_element_type=F32
    )


def row_ids(rows, cols):
    return lax.broadcasted_iota(jnp.int32, (rows, cols), 0)


def fetch(pairs, sems):
    copies = [pltpu.make_async_copy(a, b, sems.at[i]) for i, (a, b) in enumerate(pairs)]
    for copy in copies:
        copy.start()
    for copy in copies:
        copy.wait()


def prepare(
    count_ref, kappa_ref, gc_any, vert_any, thick_any, flux_any, part_any, slot_any, weight_any,
    nbr_any, payload_ref, misc_ref,
    gc_ref, vert_ref, thick_ref, flux_ref, part_ref, slot_ref, weight_ref, nbr_ref, sems,
):
    fetch(
        [
            (gc_any, gc_ref),
            (vert_any, vert_ref),
            (thick_any, thick_ref),
            (flux_any, flux_ref),
            (part_any, part_ref),
            (slot_any, slot_ref),
            (weight_any, weight_ref),
            (nbr_any, nbr_ref),
        ],
        sems,
    )
    tiles, block_rows, col_max = payload_ref.shape
    species, layers, _ = vert_ref.shape
    width = species * layers
    v = vert_ref[...].astype(F32).reshape(width, layers)
    v = jnp.concatenate([v] * species, axis=1)
    rows = row_ids(width, width) // layers
    cols = lax.broadcasted_iota(jnp.int32, (width, width), 1) // layers
    vt = jnp.where(rows == cols, v, 0.0).T
    hi = lax.Precision.HIGHEST
    v2 = nn(vt, vt, hi)
    v4 = nn(v2, v2, hi)
    th = jnp.concatenate([thick_ref[s : s + 1, :] for s in range(species)], axis=1)
    misc_ref[0:8] = nt(jnp.broadcast_to(th, (8, width)), v4, hi)
    rates = [jnp.full((1, width), kappa_ref[s], F32) for s in range(species)]
    misc_ref[8:16] = jnp.concatenate(rates + rates, axis=0)
    live = lax.broadcasted_iota(jnp.int32, (1, col_max), 1) < count_ref[0]
    w = jnp.where(live, nt(v4.astype(BF16), gc_ref[...]), 0.0)
    slot, nbr = slot_ref[...], nbr_ref[...]
    power = (slot // WIDE) * 8 + jnp.where(live, nbr // WIDE, DEAD)
    code = 128.0 + part_ref[...].astype(F32)
    for bit in range(5):
        code = code * jnp.where((power >> bit) & 1 == 1, float(2 ** (2**bit)), 1.0)
    common = [(slot % WIDE).astype(F32), (nbr % WIDE).astype(F32), code]
    common = jnp.concatenate(common, axis=0)
    own = width // tiles
    pad = [] if own == OWN else [jnp.zeros((OWN - own, col_max), F32)]
    flux, weight = flux_ref[...], weight_ref[...]
    for q in range(tiles):
        s = q * own // layers
        pieces = [w[q * own : (q + 1) * own]] + pad + [flux[s : s + 1] * weight, common]
        payload_ref[q] = jnp.concatenate(pieces, axis=0).astype(BF16)


def decoded(code):
    power = jnp.zeros(code.shape, jnp.int32)
    for bit in (16, 8, 4, 2, 1):
        large = code >= 128.0 * 2.0**bit
        code = jnp.where(large, code * 2.0**-bit, code)
        power = power + jnp.where(large, bit, 0)
    return code - 128.0, power


def hot(key, ids):
    return jnp.where(ids == key, jnp.ones((), BF16), jnp.zeros((), BF16))


def picked(keys, value, target):
    return jnp.where(keys == jnp.asarray(target, BF16), value, jnp.zeros((), BF16))


def narrow(ints):
    return ints.astype(F32).astype(BF16)


def each(count, step):
    if count <= 8:
        for q in range(count):
            step(q, 0)
    else:
        lax.fori_loop(0, count, step, 0)


def chain(tiles, own, layers, keep, misc_ref, data_ref, *refs):
    back_ref, rest = refs[0], refs[1:]
    if not keep:
        y_ref, rest = rest[0], rest[1:]
    x_ref, table_ref, hot_ref = rest
    col_max = data_ref.shape[2]
    blocks = col_max // LANES
    me = lax.axis_index("tile")
    ids = narrow(row_ids(LANES, 1))
    half = row_ids(16, 1) // blocks
    within = row_ids(16, 1) % blocks

    table_ref[...] = jnp.zeros_like(table_ref)

    def gather(q, carry):
        block = data_ref[q].astype(F32)
        part, power = decoded(block[OWN + 12 : OWN + 16])
        low = block[OWN + 4 : OWN + 8].astype(jnp.int32)
        sub = (power >> 3) * 2 + (low >> 7)
        low = narrow(low & 127)
        total = jnp.zeros(table_ref.shape, F32)
        for r in range(4):
            value = block[OWN + r : OWN + r + 1]
            value = jnp.broadcast_to(value, (16, col_max)).astype(BF16)
            key = jnp.where(sub[r : r + 1] == within, part[r : r + 1] - half.astype(F32), -3.0)
            key = key.astype(BF16)
            rows = jnp.concatenate([picked(key, value, 2 * g) for g in range(tiles // 2)], axis=0)
            total = total + nt(rows, hot(low[r : r + 1], ids))
        table_ref[...] += total
        return carry

    each(tiles, gather)

    lane = lax.broadcasted_iota(jnp.int32, (OWN, misc_ref.shape[1]), 1)
    row = row_ids(OWN, 1)
    tv_own = jnp.sum(
        jnp.where((lane == me * own + row) & (row < own), misc_ref[0:1], 0.0), axis=1, keepdims=True
    )
    mine = me * own // layers
    rate = jnp.zeros((1, 1), F32)
    for s in range(4):
        rate = jnp.where(mine == s, misc_ref[8 + s : 9 + s, 0:1], rate)

    def start(q, carry):
        block = data_ref[q].astype(F32)
        live = decoded(block[OWN + 12 : OWN + 13])[1] & 7 != DEAD
        piece = table_ref[pl.ds(q * blocks, blocks), :]
        inj = jnp.concatenate([piece[h : h + 1] for h in range(blocks)], axis=1)
        x_ref[0, q] = block[0:OWN] + tv_own * jnp.where(live, inj, 0.0)
        return carry

    each(tiles, start)

    for step in range(SUB):
        here, there = step % 2, (step + 1) % 2
        for q in range(tiles):
            x_ref[there, q] = (1.0 - 4.0 * rate) * x_ref[here, q]

        def apply(q, carry):
            block = data_ref[q].astype(F32)
            low = block[OWN + 8 : OWN + 12].astype(jnp.int32)
            high = (decoded(block[OWN + 12 : OWN + 16])[1] & 7) * 2 + (low >> 7)
            value = (rate * x_ref[here, q]).astype(BF16)
            total = jnp.zeros(((blocks + 2) * OWN, LANES), F32)
            for n in range(4):
                key = narrow(jnp.broadcast_to(high[n : n + 1], (OWN, col_max)))
                rows = [picked(key, value, h) for h in range(blocks + 2)]
                if not keep or step == 0:
                    ones = hot(narrow(low[n : n + 1] & 127), ids)
                else:
                    ones = hot_ref[q * 4 + n]
                if keep and step == 0:
                    hot_ref[q * 4 + n] = ones
                total = total + nt(jnp.concatenate(rows, axis=0), ones)
            mine_rows = [total[h * OWN : (h + 1) * OWN] for h in range(blocks)]
            x_ref[there, q] += jnp.concatenate(mine_rows, axis=1)
            cross = [total[(blocks + k) * OWN : (blocks + k + 1) * OWN] for k in range(2)]
            if isinstance(q, int):
                if q > 0:
                    x_ref[there, q - 1, :, LANES : 2 * LANES] += cross[0]
                if q < tiles - 1:
                    x_ref[there, q + 1, :, :LANES] += cross[1]
            else:
                before, after = jnp.maximum(q - 1, 0), jnp.minimum(q + 1, tiles - 1)
                x_ref[there, before, :, LANES : 2 * LANES] += jnp.where(q > 0, cross[0], 0.0)
                x_ref[there, after, :, :LANES] += jnp.where(q < tiles - 1, cross[1], 0.0)
            return carry

        each(tiles, apply)
    last = SUB % 2
    top = jnp.concatenate([x_ref[last, q, 0:1] for q in range(tiles)], axis=0)
    for q in range(tiles):
        if keep:
            back_ref[q] = jnp.concatenate([x_ref[last, q], top], axis=0).astype(BF16)
        else:
            back_ref[q] = x_ref[last, q, 0:own].astype(BF16)
    if not keep:
        y_ref[...] = top


def gather_bottom(
    tiles, keep, y_ref, part_any, slot_any, weight_any, out_ref, found_ref,
    part_ref, slot_ref, weight_ref, sems,
):
    fetch([(part_any, part_ref), (slot_any, slot_ref), (weight_any, weight_ref)], sems)
    col_max = part_ref.shape[1]
    subs = col_max // WIDE
    table = []
    for s in range(4):
        y = (y_ref[s * tiles // 4].astype(F32)[OWN:] if keep else y_ref[s].astype(F32))
        table += [y[:, h * WIDE : (h + 1) * WIDE] for h in range(subs)]
    table = jnp.concatenate(table, axis=0).astype(BF16)
    slot, part = slot_ref[...], part_ref[...]
    sub = slot // WIDE
    low = narrow(slot % WIDE)
    ids = narrow(row_ids(WIDE, 1))
    places = row_ids(tiles, 1)
    totals = [jnp.zeros((tiles, col_max), F32) for s in range(4)]
    for r in range(4):
        found_ref[...] = nn(table, hot(low[r : r + 1], ids))
        key = jnp.where(part[r : r + 1] == places, sub[r : r + 1], -1)
        weight = weight_ref[r : r + 1, :]
        for s in range(4):
            found = jnp.zeros((tiles, col_max), F32)
            for h in range(subs):
                at = (s * subs + h) * tiles
                found = jnp.where(key == h, found_ref[at : at + tiles, :], found)
            totals[s] = totals[s] + found * weight
    rows = [jnp.sum(total, axis=0, keepdims=True) for total in totals]
    rows.append(jnp.zeros((out_ref.shape[0] - 4, col_max), F32))
    out_ref[...] = jnp.concatenate(rows, axis=0).astype(BF16)


def combine(layers, reaction_ref, all_ref, tail_ref, state_ref, bottom_ref):
    parts, wide, col_max = all_ref.shape
    out_species, species = reaction_ref.shape
    own = species // parts
    width = out_species * layers
    mix = reaction_ref[...].astype(BF16)
    left = jnp.where(
        row_ids(width, out_species) // layers
        == lax.broadcasted_iota(jnp.int32, (width, out_species), 1),
        1.0,
        0.0,
    ).astype(BF16)
    right = jnp.where(
        row_ids(species, species * layers)
        == lax.broadcasted_iota(jnp.int32, (species, species * layers), 1) // layers,
        1.0,
        0.0,
    ).astype(BF16)
    full = nn(nn(left, mix).astype(BF16), right)
    same = (
        row_ids(width, species * layers) % layers
        == lax.broadcasted_iota(jnp.int32, (width, species * layers), 1) % layers
    )
    full = jnp.where(same, full, 0.0).astype(BF16)
    mixed = jnp.zeros((width, col_max), F32)
    bottom = jnp.zeros((out_species, col_max), F32)
    mix = mix.astype(F32)
    for k in range(parts):
        mixed = mixed + nn(full[:, k * wide : (k + 1) * wide], all_ref[k])
        tail = tail_ref[k].astype(F32)
        for s in range(own):
            col = k * own + s
            bottom = bottom + mix[:, col : col + 1] * tail[s : s + 1, :]
    state_ref[...] = mixed.T.astype(BF16)
    bottom_ref[...] = bottom


def body(
    grad_columns,
    grad_flux,
    remap_part,
    remap_slot,
    remap_weight,
    col_count,
    neighbors,
    kappa,
    thickness,
    vertical,
    reaction,
):
    tiles = lax.axis_size("tile")
    col_max, width = grad_columns.shape
    layers = thickness.shape[1]
    own = width // tiles
    entries = tiles * col_max // WIDE
    part_t, slot_t, weight_t, nbr_t = remap_part.T, remap_slot.T, remap_weight.T, neighbors.T
    shape = jax.ShapeDtypeStruct
    moved = [grad_columns, vertical, thickness, grad_flux, part_t, slot_t, weight_t, nbr_t]
    payload, misc = call(
        prepare,
        [shape((tiles, OWN + 16, col_max), BF16), shape((16, width), F32)],
        [SMEM] * 2 + [HBM] * 8,
        scratch=[pltpu.VMEM(a.shape, a.dtype) for a in moved] + [pltpu.SemaphoreType.DMA((8,))],
        flops=4 * 10**7,
        moved=10**6,
        limit=MOST,
    )(col_count, kappa, *moved)
    data = lax.all_to_all(payload, "tile", split_axis=0, concat_axis=0, tiled=True)
    keep = tiles == 8
    sent = OWN + tiles if keep else own
    backs = [shape((tiles, sent, col_max), BF16)]
    if not keep:
        backs.append(shape((tiles, col_max), F32))
    back = call(
        functools.partial(chain, tiles, own, layers, keep),
        backs,
        [VMEM] * 2,
        scratch=[
            pltpu.VMEM((2, tiles, OWN, col_max), F32),
            pltpu.VMEM((tiles * col_max // LANES, LANES), F32),
            pltpu.VMEM((tiles * 4 if keep else 1, LANES, col_max), BF16),
        ],
        flops=10**10,
        moved=10**6,
    )(misc, data)
    home = lax.all_to_all(back[0], "tile", split_axis=0, concat_axis=0, tiled=True)
    if keep:
        y = home
    else:
        place = lax.axis_index("tile") * own
        mark = jnp.arange(4)[:, None, None] * layers == place
        y = lax.psum(jnp.where(mark, back[1][None], 0.0).astype(BF16), "tile")
    remaps = [part_t, slot_t, weight_t]
    bottom = call(
        functools.partial(gather_bottom, tiles, keep),
        [shape((16, col_max), BF16)],
        [VMEM] + [HBM] * 3,
        scratch=[pltpu.VMEM((entries * 4, col_max), F32)]
        + [pltpu.VMEM(a.shape, a.dtype) for a in remaps]
        + [pltpu.SemaphoreType.DMA((3,))],
        flops=10**9,
        moved=10**6,
    )(y, *remaps)[0]
    every_bottom = lax.all_gather(bottom, "spec", axis=0, tiled=False)
    every = lax.all_gather(home[:, :own].reshape(width, col_max), "spec", axis=0, tiled=False)
    grad_state, grad_bottom = call(
        functools.partial(combine, layers),
        [shape((col_max, width), BF16), shape((reaction.shape[1], col_max), F32)],
        [VMEM] * 3,
        flops=2 * 10**8,
        moved=2 * 10**6,
    )(reaction.T, every, every_bottom)
    return grad_state, grad_bottom


def solution(mesh):
    placed = (
        P("tile", "spec"),
        P("spec", "tile"),
        P("tile", None),
        P("tile", None),
        P("tile", None),
        P("tile"),
        P("tile", None),
        P("spec"),
        P("spec", None),
        P("spec", None, None),
        P(None, "spec"),
    )
    return jax.shard_map(
        body,
        mesh=mesh,
        in_specs=placed,
        out_specs=(P("tile", "spec"), P("spec", "tile")),
        check_vma=False,
    )
```

time: 114 us -> 95.1 us (0.83)
  Pallas kernels: 37.5 us -> 25.3 us
  local copies, waits for them, and re-layouts: 9.25 us -> 3.35 us
    pallas_call x3, Pallas kernels: 36.1 us -> 23.9 us  [the longest x1 20 us: body(): call(functools.partial(chain, tiles, own, layers, keep), backs, [VMEM] *...]
    unnamed x28 -> x12, local copies, waits for them, and re-layouts: 9.25 us -> 2.63 us
    all_to_all x1, blocking collectives: 11.9 us -> 15.1 us  [body(): lax.all_to_all(back[0], 'tile', split_axis=0, concat_axis=0, tiled=True)]
    all_to_all x1, blocking collectives: 24.8 us -> 21.8 us  [body(): lax.all_to_all(payload, 'tile', split_axis=0, concat_axis=0, tiled=True)]
  transfers between devices with their start and end apart: 1 -> 1, of which waited for: 1 -> 1; matrix products, arithmetic and copies ran while one was open for 0% -> 0% of each run, Pallas kernels for 0% -> 1%
where the time goes in v3:
time: 95.1 us; the launch traced here: 94.6 us
  blocking collectives  42.4 us (45%)
  Pallas kernels  25.3 us (27%)
  between operations  14.7 us (15%)
  waiting for transfers between devices  8.83 us (9%)
  local copies, waits for them, and re-layouts  3.35 us (4%)
    all_to_all x1, blocking collectives, body(): lax.all_to_all(payload, 'tile', split_axis=0, concat_axis=0, tiled=True)  21.8 us
    pallas_call x1, Pallas kernels, body(): call(functools.partial(chain, tiles, own, layers, keep), backs, [VMEM] *...  20 us
    all_to_all x1, blocking collectives, body(): lax.all_to_all(back[0], 'tile', split_axis=0, concat_axis=0, tiled=True)  15.1 us
    all_gather x1, waiting for transfers between devices, body(): lax.all_gather(home[:, :own].reshape(width, col_max), 'spec', axis=0, til...  8.81 us
    all_gather x1, blocking collectives, body(): every_bottom = lax.all_gather(bottom, 'spec', axis=0, tiled=False)  5.43 us
    pallas_call x1, Pallas kernels, body(): call(prepare, [shape((tiles, OWN + 16, col_max), BF16), shape((16, width)...  3.4 us
    unnamed x12, local copies, waits for them, and re-layouts  2.63 us
  transfers between devices with their start and end apart: 1, of which 1 were waited for; matrix products, arithmetic and copies ran while one was open for 0% of the time, Pallas kernels for 1%

profile of v3, /device:TPU:0, one launch (start us, length us, event | category | flops | bytes accessed | tf_op | source)
XLA Modules:
  0.0 94.6 jit_solution(3927829342139649735)
XLA Ops:
  7.2 0.0 all-gather.3.cloned.1.call-start
  7.9 3.4 %shard_map.122 = (bf16[8,32,1024]{2,1,0:T(8,128)(2,1)}, f32[16,128]{1,0:T(8,128)}) custom-call(s32[1]{0:T(128)S(6)} %copy.13.count_ref, f32[4]{0:T(128)} %kappa_ref.1, bf16[1024,128]{1,0:T(8,128)(2,1)} %gc_any.1, bf16[4,32,32]{2,1,0:T(8,128)(2,1)} %vert_any.1, f32[4,32]{1,0:T(4,128)} %thick_any.1, f32[4,1024]{1,0:T(4,128)} %flux_any.1, s32[4,1024]{1,0:T(4,128)} %bitcast.8, ...), custom_call_target="tpu_custom_call" | custom-call | flops 40000000 | bytes 1000000 | tf_op jit(solution)/shard_map/pallas_call | solution.py:331
  11.3 0.0 copy-start.5
  11.3 21.8 %all_to_all.10.data_ref = bf16[8,32,1024]{2,1,0:T(8,128)(2,1)S(1)} all-to-all(bf16[8,32,1024]{2,1,0:T(8,128)(2,1)} %get-tuple-element.5), channel_id=1, replica_groups=mesh['tile'=8,'spec'=4] {'tile'}, dimensions={0} | all-to-all | bytes 1048576 | tf_op jit(solution)/shard_map/all_to_all | solution.py:340
  33.1 0.0 copy-done.5
  33.1 20.0 %shard_map.123 = bf16[8,24,1024]{2,1,0:T(8,128)(2,1)S(1)} custom-call(f32[16,128]{1,0:T(8,128)S(1)} %copy-done.5, bf16[8,32,1024]{2,1,0:T(8,128)(2,1)S(1)} %all_to_all.10.data_ref), custom_call_target="tpu_custom_call" | custom-call | flops 10000000000 | bytes 1000000 | tf_op jit(solution)/shard_map/pallas_call | solution.py:346
  53.1 15.1 %all_to_all.11.y_ref = bf16[8,24,1024]{2,1,0:T(8,128)(2,1)S(1)} all-to-all(bf16[8,24,1024]{2,1,0:T(8,128)(2,1)S(1)} %shard_map.123), channel_id=1, replica_groups=mesh['tile'=8,'spec'=4] {'tile'}, dimensions={0} | all-to-all | bytes 786432 | tf_op jit(solution)/shard_map/all_to_all | solution.py:358
  68.2 0.7 slice.4
  68.9 0.0 copy-start.1
  68.9 0.0 copy-start.2
  68.9 0.0 copy-start.3
  68.9 0.0 all-gather.3.cloned.1.call-update
  69.0 0.7 copy-done.1
  69.7 0.0 copy-done.2
  69.7 0.0 copy-done.3
  69.7 0.5 shard_map.124
  70.2 5.4 %all-gather = bf16[64,1024]{1,0:T(8,128)(2,1)S(1)} all-gather(bf16[16,1024]{1,0:T(8,128)(2,1)S(1)} %shard_map.124), channel_id=2, replica_groups=mesh['tile'=8,'spec'=4] {'spec'}, dimensions={0}, use_global_device_ids=true | all-gather | bytes 163840 | tf_op jit(solution)/shard_map/all_gather | solution.py:376
  75.7 8.8 %all-gather.3.cloned.1.call-done.all_ref = bf16[4,128,1024]{2,1,0:T(8,128)(2,1)} async-done(((bf16[1,128,1024]{2,1,0:T(8,128)(2,1)}), bf16[4,128,1024]{2,1,0:T(8,128)(2,1)}) %all-gather.3.cloned.1.call-update) | async-done | bytes 1048592 | tf_op jit(solution)/shard_map/all_gather | solution.py:377
  84.5 0.0 copy-start.4
  84.5 0.7 copy-done.4
  85.2 0.0 copy-start
  85.2 1.2 %copy-done = bf16[4,128,1024]{2,1,0:T(8,128)(2,1)S(1)} copy-done((bf16[4,128,1024]{2,1,0:T(8,128)(2,1)S(1)}, bf16[4,128,1024]{2,1,0:T(8,128)(2,1)}, u32[]{:S(2)}) %copy-start) | copy-done | bytes 1048600
  86.4 1.4 %shard_map.125 = (bf16[1024,128]{1,0:T(8,128)(2,1)}, f32[4,1024]{1,0:T(4,128)}) custom-call(bf16[4,16]{1,0:T(4,128)(2,1)S(1)} %bitcast.14, bf16[4,128,1024]{2,1,0:T(8,128)(2,1)S(1)} %copy-done, bf16[4,16,1024]{2,1,0:T(8,128)(2,1)S(1)} %bitcast.7), custom_call_target="tpu_custom_call" | custom-call | flops 200000000 | bytes 2000000 | tf_op jit(solution)/shard_map/pallas_call | solution.py:378
Async XLA Ops:
  7.2 77.3 %all-gather.3.cloned.1.call-start = ((), (), s32[]{:S(2)}) async-start(), calls=%async_computation.2 | async-start | bytes 1310720 | tf_op jit(solution)/shard_map/all_gather | solution.py:377
  11.3 21.8 %copy-start.5 = (f32[16,128]{1,0:T(8,128)S(1)}, f32[16,128]{1,0:T(8,128)}, u32[]{:S(2)}) copy-start(f32[16,128]{1,0:T(8,128)} %get-tuple-element.4.misc_ref) | copy-start | bytes 24580
  68.9 0.7 copy-start.1
  68.9 0.7 copy-start.2
  68.9 0.7 copy-start.3
  84.5 0.7 copy-start.4
  85.2 1.2 %copy-start = (bf16[4,128,1024]{2,1,0:T(8,128)(2,1)S(1)}, bf16[4,128,1024]{2,1,0:T(8,128)(2,1)}, u32[]{:S(2)}) copy-start(bf16[4,128,1024]{2,1,0:T(8,128)(2,1)} %all-gather.3.cloned.1.call-done.all_ref) | copy-start | bytes 3145732
Sparse Core Ops, SparseCore 0:
  69.1 15.3 all-gather.2

commit v4 on v3

--- a/solution.py
+++ b/solution.py
@@ -59,8 +59,9 @@
 
 def prepare(
     count_ref, kappa_ref, gc_any, vert_any, thick_any, flux_any, part_any, slot_any, weight_any,
-    nbr_any, payload_ref, misc_ref,
-    gc_ref, vert_ref, thick_ref, flux_ref, part_ref, slot_ref, weight_ref, nbr_ref, sems,
+    nbr_any, reaction_any, payload_ref, misc_ref, remap_ref,
+    gc_ref, vert_ref, thick_ref, flux_ref, part_ref, slot_ref, weight_ref, nbr_ref, reaction_ref,
+    sems,
 ):
     fetch(
         [
@@ -72,6 +73,7 @@
             (slot_any, slot_ref),
             (weight_any, weight_ref),
             (nbr_any, nbr_ref),
+            (reaction_any, reaction_ref),
         ],
         sems,
     )
@@ -89,7 +91,9 @@
     th = jnp.concatenate([thick_ref[s : s + 1, :] for s in range(species)], axis=1)
     misc_ref[0:8] = nt(jnp.broadcast_to(th, (8, width)), v4, hi)
     rates = [jnp.full((1, width), kappa_ref[s], F32) for s in range(species)]
-    misc_ref[8:16] = jnp.concatenate(rates + rates, axis=0)
+    mix = reaction_ref[...].astype(F32)
+    mix = jnp.concatenate([mix, jnp.zeros((4, width - mix.shape[1]), F32)], axis=1)
+    misc_ref[8:16] = jnp.concatenate(rates + [mix], axis=0)
     live = lax.broadcasted_iota(jnp.int32, (1, col_max), 1) < count_ref[0]
     w = jnp.where(live, nt(v4.astype(BF16), gc_ref[...]), 0.0)
     slot, nbr = slot_ref[...], nbr_ref[...]
@@ -102,6 +106,8 @@
     own = width // tiles
     pad = [] if own == OWN else [jnp.zeros((OWN - own, col_max), F32)]
     flux, weight = flux_ref[...], weight_ref[...]
+    subs = (slot // WIDE).astype(F32)
+    remap_ref[...] = jnp.concatenate([common[0:4], part_ref[...].astype(F32), subs, weight], axis=0)
     for q in range(tiles):
         s = q * own // layers
         pieces = [w[q * own : (q + 1) * own]] + pad + [flux[s : s + 1] * weight, common]
@@ -237,28 +243,25 @@
         y_ref[...] = top
 
 
-def gather_bottom(
-    tiles, keep, y_ref, part_any, slot_any, weight_any, out_ref, found_ref,
-    part_ref, slot_ref, weight_ref, sems,
-):
-    fetch([(part_any, part_ref), (slot_any, slot_ref), (weight_any, weight_ref)], sems)
-    col_max = part_ref.shape[1]
+def gather_bottom(tiles, own, parts, keep, y_ref, home_ref, remap_ref, out_ref, found_ref):
+    col_max = remap_ref.shape[1]
+    width = tiles * own
     subs = col_max // WIDE
     table = []
     for s in range(4):
-        y = (y_ref[s * tiles // 4].astype(F32)[OWN:] if keep else y_ref[s].astype(F32))
+        y = y_ref[s * tiles // 4, OWN:] if keep else y_ref[s]
         table += [y[:, h * WIDE : (h + 1) * WIDE] for h in range(subs)]
-    table = jnp.concatenate(table, axis=0).astype(BF16)
-    slot, part = slot_ref[...], part_ref[...]
-    sub = slot // WIDE
-    low = narrow(slot % WIDE)
+    table = jnp.concatenate([piece.astype(F32) for piece in table], axis=0).astype(BF16)
+    low = remap_ref[0:4].astype(BF16)
+    part = remap_ref[4:8].astype(jnp.int32)
+    sub = remap_ref[8:12].astype(jnp.int32)
     ids = narrow(row_ids(WIDE, 1))
     places = row_ids(tiles, 1)
     totals = [jnp.zeros((tiles, col_max), F32) for s in range(4)]
     for r in range(4):
         found_ref[...] = nn(table, hot(low[r : r + 1], ids))
         key = jnp.where(part[r : r + 1] == places, sub[r : r + 1], -1)
-        weight = weight_ref[r : r + 1, :]
+        weight = remap_ref[12 + r : 13 + r]
         for s in range(4):
             found = jnp.zeros((tiles, col_max), F32)
             for h in range(subs):
@@ -266,16 +269,24 @@
                 found = jnp.where(key == h, found_ref[at : at + tiles, :], found)
             totals[s] = totals[s] + found * weight
     rows = [jnp.sum(total, axis=0, keepdims=True) for total in totals]
-    rows.append(jnp.zeros((out_ref.shape[0] - 4, col_max), F32))
-    out_ref[...] = jnp.concatenate(rows, axis=0).astype(BF16)
-
-
-def combine(layers, reaction_ref, all_ref, tail_ref, state_ref, bottom_ref):
-    parts, wide, col_max = all_ref.shape
-    out_species, species = reaction_ref.shape
-    own = species // parts
+    rows.append(jnp.zeros((16 - 4, col_max), F32))
+    rows = jnp.concatenate(rows, axis=0).astype(BF16)
+    for k in range(parts):
+        if keep:
+            for q in range(tiles):
+                out_ref[k, q * own : (q + 1) * own] = home_ref[q, :own]
+        else:
+            out_ref[k, :width] = home_ref[...]
+        out_ref[k, width:] = rows
+
+
+def combine(layers, misc_ref, all_ref, state_ref, bottom_ref):
+    parts, rows, col_max = all_ref.shape
+    wide = rows - 16
+    own = wide // layers
+    out_species, species = own, parts * own
     width = out_species * layers
-    mix = reaction_ref[...].astype(BF16)
+    mix = misc_ref[12 : 12 + out_species, 0:species]
     left = jnp.where(
         row_ids(width, out_species) // layers
         == lax.broadcasted_iota(jnp.int32, (width, out_species), 1),
@@ -288,7 +299,7 @@
         1.0,
         0.0,
     ).astype(BF16)
-    full = nn(nn(left, mix).astype(BF16), right)
+    full = nn(nn(left, mix.astype(BF16)).astype(BF16), right)
     same = (
         row_ids(width, species * layers) % layers
         == lax.broadcasted_iota(jnp.int32, (width, species * layers), 1) % layers
@@ -296,10 +307,9 @@
     full = jnp.where(same, full, 0.0).astype(BF16)
     mixed = jnp.zeros((width, col_max), F32)
     bottom = jnp.zeros((out_species, col_max), F32)
-    mix = mix.astype(F32)
     for k in range(parts):
-        mixed = mixed + nn(full[:, k * wide : (k + 1) * wide], all_ref[k])
-        tail = tail_ref[k].astype(F32)
+        mixed = mixed + nn(full[:, k * wide : (k + 1) * wide], all_ref[k, :wide, :])
+        tail = all_ref[k, wide:, :].astype(F32)
         for s in range(own):
             col = k * own + s
             bottom = bottom + mix[:, col : col + 1] * tail[s : s + 1, :]
@@ -321,6 +331,7 @@
     reaction,
 ):
     tiles = lax.axis_size("tile")
+    parts = lax.axis_size("spec")
     col_max, width = grad_columns.shape
     layers = thickness.shape[1]
     own = width // tiles
@@ -328,11 +339,13 @@
     part_t, slot_t, weight_t, nbr_t = remap_part.T, remap_slot.T, remap_weight.T, neighbors.T
     shape = jax.ShapeDtypeStruct
     moved = [grad_columns, vertical, thickness, grad_flux, part_t, slot_t, weight_t, nbr_t]
-    payload, misc = call(
+    moved.append(reaction.T)
+    payload, misc, remap = call(
         prepare,
-        [shape((tiles, OWN + 16, col_max), BF16), shape((16, width), F32)],
-        [SMEM] * 2 + [HBM] * 8,
-        scratch=[pltpu.VMEM(a.shape, a.dtype) for a in moved] + [pltpu.SemaphoreType.DMA((8,))],
+        [shape((tiles, OWN + 16, col_max), BF16), shape((16, width), F32)]
+        + [shape((16, col_max), F32)],
+        [SMEM] * 2 + [HBM] * 9,
+        scratch=[pltpu.VMEM(a.shape, a.dtype) for a in moved] + [pltpu.SemaphoreType.DMA((9,))],
         flops=4 * 10**7,
         moved=10**6,
         limit=MOST,
@@ -362,26 +375,23 @@
         place = lax.axis_index("tile") * own
         mark = jnp.arange(4)[:, None, None] * layers == place
         y = lax.psum(jnp.where(mark, back[1][None], 0.0).astype(BF16), "tile")
-    remaps = [part_t, slot_t, weight_t]
-    bottom = call(
-        functools.partial(gather_bottom, tiles, keep),
-        [shape((16, col_max), BF16)],
-        [VMEM] + [HBM] * 3,
-        scratch=[pltpu.VMEM((entries * 4, col_max), F32)]
-        + [pltpu.VMEM(a.shape, a.dtype) for a in remaps]
-        + [pltpu.SemaphoreType.DMA((3,))],
+        home = home.reshape(width, col_max)
+    packed = call(
+        functools.partial(gather_bottom, tiles, own, parts, keep),
+        [shape((parts, width + 16, col_max), BF16)],
+        [VMEM] * 3,
+        scratch=[pltpu.VMEM((entries * 4, col_max), F32)],
         flops=10**9,
         moved=10**6,
-    )(y, *remaps)[0]
-    every_bottom = lax.all_gather(bottom, "spec", axis=0, tiled=False)
-    every = lax.all_gather(home[:, :own].reshape(width, col_max), "spec", axis=0, tiled=False)
+    )(y, home, remap)[0]
+    every = lax.all_to_all(packed, "spec", split_axis=0, concat_axis=0, tiled=True)
     grad_state, grad_bottom = call(
         functools.partial(combine, layers),
-        [shape((col_max, width), BF16), shape((reaction.shape[1], col_max), F32)],
-        [VMEM] * 3,
+        [shape((col_max, width), BF16), shape((4, col_max), F32)],
+        [VMEM] * 2,
         flops=2 * 10**8,
         moved=2 * 10**6,
-    )(reaction.T, every, every_bottom)
+    )(misc, every)
     return grad_state, grad_bottom
 
 

time: 95.1 us -> 83.1 us (0.87)
  between operations: 14.7 us -> 1.32 us
  blocking collectives: 42.4 us -> 55.4 us
  waiting for transfers between devices: 8.83 us -> 0 us
  local copies, waits for them, and re-layouts: 3.35 us -> 0.71 us
    all_to_all x0 -> x1, blocking collectives: none -> 18.4 us  [body(): lax.all_to_all(packed, 'spec', split_axis=0, concat_axis=0, tiled=True)]
    all_gather x1 -> x0, waiting for transfers between devices: 8.81 us -> none  [body(): lax.all_gather(home[:, :own].reshape(width, col_max), 'spec', axis=0, til...]
    all_gather x1 -> x0, blocking collectives: 5.43 us -> none  [body(): every_bottom = lax.all_gather(bottom, 'spec', axis=0, tiled=False)]
    unnamed x12 -> x6, local copies, waits for them, and re-layouts: 2.63 us -> 0.71 us
  transfers between devices with their start and end apart: 1 -> 0, of which waited for: 1 -> 0; matrix products, arithmetic and copies ran while one was open for 0% -> 0% of each run, Pallas kernels for 1% -> 0%
where the time goes in v4:
time: 83.1 us; the launch traced here: 82.7 us
  blocking collectives  55.4 us (67%)
  Pallas kernels  25.3 us (30%)
  between operations  1.32 us (2%)
    all_to_all x1, blocking collectives, body(): lax.all_to_all(payload, 'tile', split_axis=0, concat_axis=0, tiled=True)  21.8 us
    pallas_call x1, Pallas kernels, body(): call(functools.partial(chain, tiles, own, layers, keep), backs, [VMEM] *...  20 us
    all_to_all x1, blocking collectives, body(): lax.all_to_all(packed, 'spec', split_axis=0, concat_axis=0, tiled=True)  18.4 us
    all_to_all x1, blocking collectives, body(): lax.all_to_all(back[0], 'tile', split_axis=0, concat_axis=0, tiled=True)  15.1 us
    pallas_call x1, Pallas kernels, body(): call(prepare, [shape((tiles, OWN + 16, col_max), BF16), shape((16, width)...  3.42 us

profile of v4, /device:TPU:0, one launch (start us, length us, event | category | flops | bytes accessed | tf_op | source)
XLA Modules:
  0.0 82.7 jit_solution(10686085080193651458)
XLA Ops:
  1.3 3.4 %shard_map.122 = (bf16[8,32,1024]{2,1,0:T(8,128)(2,1)}, f32[16,128]{1,0:T(8,128)}, f32[16,1024]{1,0:T(8,128)}) custom-call(s32[1]{0:T(128)S(6)} %copy.13.count_ref, f32[4]{0:T(128)} %kappa_ref.1, bf16[1024,128]{1,0:T(8,128)(2,1)} %gc_any.1, bf16[4,32,32]{2,1,0:T(8,128)(2,1)} %vert_any.1, f32[4,32]{1,0:T(4,128)} %thick_any.1, f32[4,1024]{1,0:T(4,128)} %flux_any.1, ...), custom_call_target="tpu_custom_call" | custom-call | flops 40000000 | bytes 1000000 | tf_op jit(solution)/shard_map/pallas_call | solution.py:343
  4.7 21.8 %all_to_all.15.data_ref = bf16[8,32,1024]{2,1,0:T(8,128)(2,1)S(1)} all-to-all(bf16[8,32,1024]{2,1,0:T(8,128)(2,1)} %get-tuple-element.6), channel_id=1, replica_groups=mesh['tile'=8,'spec'=4] {'tile'}, dimensions={0} | all-to-all | bytes 1048576 | tf_op jit(solution)/shard_map/all_to_all | solution.py:353
  26.5 0.0 copy-start
  26.5 0.7 copy-done
  27.2 0.0 copy-start.2
  27.2 20.0 %shard_map.123 = bf16[8,24,1024]{2,1,0:T(8,128)(2,1)S(1)} custom-call(f32[16,128]{1,0:T(8,128)S(1)} %copy-done, bf16[8,32,1024]{2,1,0:T(8,128)(2,1)S(1)} %all_to_all.15.data_ref), custom_call_target="tpu_custom_call" | custom-call | flops 10000000000 | bytes 1000000 | tf_op jit(solution)/shard_map/pallas_call | solution.py:359
  47.2 15.1 %all_to_all.16.y_ref.home_ref = bf16[8,24,1024]{2,1,0:T(8,128)(2,1)S(1)} all-to-all(bf16[8,24,1024]{2,1,0:T(8,128)(2,1)S(1)} %shard_map.123), channel_id=1, replica_groups=mesh['tile'=8,'spec'=4] {'tile'}, dimensions={0} | all-to-all | bytes 786432 | tf_op jit(solution)/shard_map/all_to_all | solution.py:371
  62.3 0.0 copy-done.2
  62.3 0.5 shard_map.124
  62.9 0.0 copy-start.1
  62.9 18.4 %all_to_all.17.all_ref = bf16[4,144,1024]{2,1,0:T(8,128)(2,1)S(1)} all-to-all(bf16[4,144,1024]{2,1,0:T(8,128)(2,1)S(1)} %shard_map.124), channel_id=1, replica_groups=mesh['tile'=8,'spec'=4] {'spec'}, dimensions={0} | all-to-all | bytes 2359296 | tf_op jit(solution)/shard_map/all_to_all | solution.py:387
  81.3 0.0 copy-done.1
  81.3 1.4 %shard_map.125 = (bf16[1024,128]{1,0:T(8,128)(2,1)}, f32[4,1024]{1,0:T(4,128)}) custom-call(f32[16,128]{1,0:T(8,128)S(1)} %copy-done.1, bf16[4,144,1024]{2,1,0:T(8,128)(2,1)S(1)} %all_to_all.17.all_ref), custom_call_target="tpu_custom_call" | custom-call | flops 200000000 | bytes 2000000 | tf_op jit(solution)/shard_map/pallas_call | solution.py:388
Async XLA Ops:
  26.5 0.7 copy-start
  27.2 35.1 %copy-start.2 = (f32[16,1024]{1,0:T(8,128)S(1)}, f32[16,1024]{1,0:T(8,128)}, u32[]{:S(2)}) copy-start(f32[16,1024]{1,0:T(8,128)} %get-tuple-element.7.remap_ref) | copy-start | bytes 196612
  62.9 18.4 %copy-start.1 = (f32[16,128]{1,0:T(8,128)S(1)}, f32[16,128]{1,0:T(8,128)}, u32[]{:S(2)}) copy-start(f32[16,128]{1,0:T(8,128)} %get-tuple-element.5.misc_ref) | copy-start | bytes 24580

commit v5 on v4

--- a/solution.py
+++ b/solution.py
@@ -233,23 +233,94 @@
 
         each(tiles, apply)
     last = SUB % 2
-    top = jnp.concatenate([x_ref[last, q, 0:1] for q in range(tiles)], axis=0)
-    for q in range(tiles):
-        if keep:
-            back_ref[q] = jnp.concatenate([x_ref[last, q], top], axis=0).astype(BF16)
-        else:
+    if not keep:
+        for q in range(tiles):
             back_ref[q] = x_ref[last, q, 0:own].astype(BF16)
-    if not keep:
-        y_ref[...] = top
-
-
-def gather_bottom(tiles, own, parts, keep, y_ref, home_ref, remap_ref, out_ref, found_ref):
+            y_ref[q : q + 1] = x_ref[last, q, 0:1]
+        return
+    quarters = col_max // WIDE
+    mix = jnp.concatenate([misc_ref[8:16], misc_ref[8:16]], axis=1)[4:8]
+    mix = jnp.concatenate([mix, mix], axis=0)
+    for g in range(quarters):
+        top = [
+            x_ref[last, tiles // quarters * g + h, 0:1, k * WIDE : (k + 1) * WIDE]
+            for h in range(tiles // quarters)
+            for k in range(quarters)
+        ]
+        top = jnp.where((me * own) % layers == 0, jnp.concatenate(top, axis=0), mix)
+        for q in range(tiles):
+            piece = x_ref[last, q, :, g * WIDE : (g + 1) * WIDE]
+            back_ref[q * quarters + g] = jnp.concatenate([piece, top], axis=0).astype(BF16)
+
+
+def middle(tiles, parts, layers, data_ref, remap_ref, out_ref):
+    col_max = remap_ref.shape[1]
+    quarters = col_max // WIDE
+    halves = layers // OWN
+    species = 4 * parts
+    me = lax.axis_index("spec")
+
+    def source(s, half):
+        return ((s % 4) * halves + half) * parts + s // 4
+
+    mix = [data_ref[source(4 * k, 1), OWN:].astype(F32)[0:4, 0:species] for k in range(parts)]
+    mix = jnp.concatenate(mix, axis=0)
+    size = species * OWN
+    left = row_ids(size, species) // OWN == lax.broadcasted_iota(jnp.int32, (size, species), 1)
+    right = row_ids(species, size) == lax.broadcasted_iota(jnp.int32, (species, size), 1) // OWN
+    left, right = (jnp.where(hit, 1.0, 0.0).astype(BF16) for hit in (left, right))
+    full = nn(nn(left, mix.astype(BF16)).astype(BF16), right)
+    same = row_ids(size, size) % OWN == lax.broadcasted_iota(jnp.int32, (size, size), 1) % OWN
+    full = jnp.where(same, full, 0.0).astype(BF16)
+    mixed = []
+    for half in range(halves):
+        x = [data_ref[source(s, half), 0:OWN] for s in range(species)]
+        mixed.append(nn(full, jnp.concatenate(x, axis=0)))
+
+    table = [data_ref[source(s, 0), OWN:].astype(F32) for s in range(species)]
+    table = jnp.concatenate(table, axis=0).astype(BF16)
+    low = remap_ref[0:4].astype(BF16)
+    place = remap_ref[4:8].astype(jnp.int32) * quarters + remap_ref[8:12].astype(jnp.int32)
+    place = place - me * tiles
+    ids = narrow(row_ids(WIDE, 1))
+    totals = [jnp.zeros((tiles, col_max), F32) for s in range(species)]
+    for r in range(4):
+        found = nn(table, hot(low[r : r + 1], ids))
+        weight = jnp.where(
+            place[r : r + 1] == row_ids(tiles, 1), remap_ref[12 + r : 13 + r], 0.0
+        )
+        for s in range(species):
+            totals[s] = totals[s] + found[s * tiles : (s + 1) * tiles] * weight
+    bottom = [jnp.sum(total, axis=0, keepdims=True) for total in totals]
+    bottom = nn(mix, jnp.concatenate(bottom, axis=0), lax.Precision.HIGHEST)
+    for k in range(parts):
+        rows = []
+        for t in range(4 * k, 4 * k + 4):
+            rows += [mixed[half][t * OWN : (t + 1) * OWN] for half in range(halves)]
+        mine = bottom[4 * k : 4 * k + 4]
+        rows += [mine[:, h * WIDE : (h + 1) * WIDE] for h in range(quarters)]
+        out_ref[k] = jnp.concatenate(rows, axis=0).astype(BF16)
+
+
+def settle(all_ref, state_ref, bottom_ref):
+    parts, rows, wide = all_ref.shape
+    width = state_ref.shape[1]
+    total = jnp.zeros((rows - width, wide), F32)
+    for k in range(parts):
+        state = all_ref[k, 0:width].astype(F32)
+        state_ref[k * wide : (k + 1) * wide, :] = state.T.astype(BF16)
+        total = total + all_ref[k, width:].astype(F32)
+    pieces = [total[h * 4 : h * 4 + 4] for h in range(parts)]
+    bottom_ref[...] = jnp.concatenate(pieces, axis=1)
+
+
+def gather_bottom(tiles, own, parts, y_ref, home_ref, remap_ref, out_ref, found_ref):
     col_max = remap_ref.shape[1]
     width = tiles * own
     subs = col_max // WIDE
     table = []
     for s in range(4):
-        y = y_ref[s * tiles // 4, OWN:] if keep else y_ref[s]
+        y = y_ref[s]
         table += [y[:, h * WIDE : (h + 1) * WIDE] for h in range(subs)]
     table = jnp.concatenate([piece.astype(F32) for piece in table], axis=0).astype(BF16)
     low = remap_ref[0:4].astype(BF16)
@@ -272,11 +343,7 @@
     rows.append(jnp.zeros((16 - 4, col_max), F32))
     rows = jnp.concatenate(rows, axis=0).astype(BF16)
     for k in range(parts):
-        if keep:
-            for q in range(tiles):
-                out_ref[k, q * own : (q + 1) * own] = home_ref[q, :own]
-        else:
-            out_ref[k, :width] = home_ref[...]
+        out_ref[k, :width] = home_ref[...]
         out_ref[k, width:] = rows
 
 
@@ -351,11 +418,12 @@
         limit=MOST,
     )(col_count, kappa, *moved)
     data = lax.all_to_all(payload, "tile", split_axis=0, concat_axis=0, tiled=True)
-    keep = tiles == 8
-    sent = OWN + tiles if keep else own
-    backs = [shape((tiles, sent, col_max), BF16)]
-    if not keep:
-        backs.append(shape((tiles, col_max), F32))
+    quarters = col_max // WIDE
+    keep = tiles == 8 and parts == quarters and layers == 2 * own and own == OWN
+    if keep:
+        backs = [shape((tiles * parts, OWN + tiles, WIDE), BF16)]
+    else:
+        backs = [shape((tiles, own, col_max), BF16), shape((tiles, col_max), F32)]
     back = call(
         functools.partial(chain, tiles, own, layers, keep),
         backs,
@@ -368,26 +436,34 @@
         flops=10**10,
         moved=10**6,
     )(misc, data)
+    outs = [shape((col_max, width), BF16), shape((4, col_max), F32)]
+    if keep:
+        home = lax.all_to_all(back[0], ("tile", "spec"), split_axis=0, concat_axis=0, tiled=True)
+        packed = call(
+            functools.partial(middle, tiles, parts, layers),
+            [shape((parts, width + OWN, WIDE), BF16)],
+            [VMEM] * 2,
+            flops=10**9,
+            moved=10**6,
+        )(home, remap)[0]
+        every = lax.all_to_all(packed, "spec", split_axis=0, concat_axis=0, tiled=True)
+        return tuple(call(settle, outs, [VMEM], flops=10**8, moved=10**6)(every))
     home = lax.all_to_all(back[0], "tile", split_axis=0, concat_axis=0, tiled=True)
-    if keep:
-        y = home
-    else:
-        place = lax.axis_index("tile") * own
-        mark = jnp.arange(4)[:, None, None] * layers == place
-        y = lax.psum(jnp.where(mark, back[1][None], 0.0).astype(BF16), "tile")
-        home = home.reshape(width, col_max)
+    place = lax.axis_index("tile") * own
+    mark = jnp.arange(4)[:, None, None] * layers == place
+    y = lax.psum(jnp.where(mark, back[1][None], 0.0).astype(BF16), "tile")
     packed = call(
-        functools.partial(gather_bottom, tiles, own, parts, keep),
-        [shape((parts, width + 16, col_max), BF16)],
+        functools.partial(gather_bottom, tiles, own, parts),
+        [shape((parts, width + OWN, col_max), BF16)],
         [VMEM] * 3,
         scratch=[pltpu.VMEM((entries * 4, col_max), F32)],
         flops=10**9,
         moved=10**6,
-    )(y, home, remap)[0]
+    )(y, home.reshape(width, col_max), remap)[0]
     every = lax.all_to_all(packed, "spec", split_axis=0, concat_axis=0, tiled=True)
     grad_state, grad_bottom = call(
         functools.partial(combine, layers),
-        [shape((col_max, width), BF16), shape((4, col_max), F32)],
+        outs,
         [VMEM] * 2,
         flops=2 * 10**8,
         moved=2 * 10**6,

time: 83.1 us -> 74.1 us (0.89)
  blocking collectives: 55.4 us -> 47.2 us
    all_to_all x1, blocking collectives: 18.4 us -> 8.76 us  [body(): lax.all_to_all(packed, 'spec', split_axis=0, concat_axis=0, tiled=True)]
    all_to_all x1, blocking collectives: 15.1 us -> 16.6 us  [body(): lax.all_to_all(back[0], ('tile', 'spec'), split_axis=0, concat_axis=0, ti...]
where the time goes in v5:
time: 74.1 us; the launch traced here: 73.7 us
  blocking collectives  47.2 us (64%)
  Pallas kernels  25.2 us (34%)
  between operations  1.31 us (2%)
    all_to_all x1, blocking collectives, body(): lax.all_to_all(payload, 'tile', split_axis=0, concat_axis=0, tiled=True)  21.8 us
    pallas_call x1, Pallas kernels, body(): call(functools.partial(chain, tiles, own, layers, keep), backs, [VMEM] *...  20 us
    all_to_all x1, blocking collectives, body(): lax.all_to_all(back[0], ('tile', 'spec'), split_axis=0, concat_axis=0, ti...  16.6 us
    all_to_all x1, blocking collectives, body(): lax.all_to_all(packed, 'spec', split_axis=0, concat_axis=0, tiled=True)  8.76 us
    pallas_call x1, Pallas kernels, body(): call(prepare, [shape((tiles, OWN + 16, col_max), BF16), shape((16, width)...  3.42 us

profile of v5, /device:TPU:0, one launch (start us, length us, event | category | flops | bytes accessed | tf_op | source)
XLA Modules:
  0.0 73.7 jit_solution(3600597122696918228)
XLA Ops:
  1.3 3.4 %shard_map.122 = (bf16[8,32,1024]{2,1,0:T(8,128)(2,1)}, f32[16,128]{1,0:T(8,128)}, f32[16,1024]{1,0:T(8,128)}) custom-call(s32[1]{0:T(128)S(6)} %copy.13.count_ref, f32[4]{0:T(128)} %kappa_ref.1, bf16[1024,128]{1,0:T(8,128)(2,1)} %gc_any.1, bf16[4,32,32]{2,1,0:T(8,128)(2,1)} %vert_any.1, f32[4,32]{1,0:T(4,128)} %thick_any.1, f32[4,1024]{1,0:T(4,128)} %flux_any.1, ...), custom_call_target="tpu_custom_call" | custom-call | flops 40000000 | bytes 1000000 | tf_op jit(solution)/shard_map/pallas_call | solution.py:410
  4.7 0.0 copy-start.1
  4.7 21.8 %all_to_all.15.data_ref = bf16[8,32,1024]{2,1,0:T(8,128)(2,1)S(1)} all-to-all(bf16[8,32,1024]{2,1,0:T(8,128)(2,1)} %get-tuple-element.6), channel_id=1, replica_groups=mesh['tile'=8,'spec'=4] {'tile'}, dimensions={0} | all-to-all | bytes 1048576 | tf_op jit(solution)/shard_map/all_to_all | solution.py:420
  26.5 0.0 copy-done.1
  26.5 20.0 %shard_map.123 = bf16[32,24,256]{2,1,0:T(8,128)(2,1)S(1)} custom-call(f32[16,128]{1,0:T(8,128)S(1)} %copy-done.1, bf16[8,32,1024]{2,1,0:T(8,128)(2,1)S(1)} %all_to_all.15.data_ref), custom_call_target="tpu_custom_call" | custom-call | flops 10000000000 | bytes 1000000 | tf_op jit(solution)/shard_map/pallas_call | solution.py:427
  46.5 0.0 copy-start
  46.5 16.6 %all_to_all.16.data_ref = bf16[32,24,256]{2,1,0:T(8,128)(2,1)S(1)} all-to-all(bf16[32,24,256]{2,1,0:T(8,128)(2,1)S(1)} %shard_map.123), channel_id=1, replica_groups=mesh['tile'=8,'spec'=4] {'tile','spec'}, dimensions={0} | all-to-all | bytes 786432 | tf_op jit(solution)/shard_map/all_to_all | solution.py:441
  63.1 0.0 copy-done
  63.1 1.0 %shard_map.124 = bf16[4,144,256]{2,1,0:T(8,128)(2,1)S(1)} custom-call(bf16[32,24,256]{2,1,0:T(8,128)(2,1)S(1)} %all_to_all.16.data_ref, f32[16,1024]{1,0:T(8,128)S(1)} %copy-done), custom_call_target="tpu_custom_call" | custom-call | flops 1000000000 | bytes 1000000 | tf_op jit(solution)/shard_map/pallas_call | solution.py:442
  64.1 8.8 %all_to_all.17.all_ref = bf16[4,144,256]{2,1,0:T(8,128)(2,1)S(1)} all-to-all(bf16[4,144,256]{2,1,0:T(8,128)(2,1)S(1)} %shard_map.124), channel_id=1, replica_groups=mesh['tile'=8,'spec'=4] {'spec'}, dimensions={0} | all-to-all | bytes 589824 | tf_op jit(solution)/shard_map/all_to_all | solution.py:449
  72.9 0.8 %shard_map.125 = (bf16[1024,128]{1,0:T(8,128)(2,1)}, f32[4,1024]{1,0:T(4,128)}) custom-call(bf16[4,144,256]{2,1,0:T(8,128)(2,1)S(1)} %all_to_all.17.all_ref), custom_call_target="tpu_custom_call" | custom-call | flops 100000000 | bytes 1000000 | tf_op jit(solution)/shard_map/pallas_call | solution.py:450
Async XLA Ops:
  4.7 21.8 %copy-start.1 = (f32[16,128]{1,0:T(8,128)S(1)}, f32[16,128]{1,0:T(8,128)}, u32[]{:S(2)}) copy-start(f32[16,128]{1,0:T(8,128)} %get-tuple-element.5.misc_ref) | copy-start | bytes 24580
  46.5 16.6 %copy-start = (f32[16,1024]{1,0:T(8,128)S(1)}, f32[16,1024]{1,0:T(8,128)}, u32[]{:S(2)}) copy-start(f32[16,1024]{1,0:T(8,128)} %get-tuple-element.7.remap_ref) | copy-start | bytes 196612
